TPU v7x, 32 devices: a whole 2x2x4 slice. The times are simulated.
32 devices in a mesh: dp: 4 (over z), ctx: 2 (over y), tp: 4 (over x, core).
Axes of the slice: x: 2, y: 2, z: 4, core: 2. Of those that a mesh axis runs over, the one named last changes fastest.
Arguments:
- hidden_states: bfloat16 [8, 1024, 1024], P('dp', 'ctx'), may hold values from -30 to 30
- out_grad: bfloat16 [8, 1024, 1024], P('dp', 'ctx'), may hold values from -6 to 6
- w_query: bfloat16 [1024, 1024], P('dp', 'tp'), may hold values from -0.1875 to 0.1875
- w_key: bfloat16 [1024, 512], P('dp', 'tp'), may hold values from -0.1875 to 0.1875
- w_value: bfloat16 [1024, 512], P('dp', 'tp'), may hold values from -0.1875 to 0.1875
- w_out: bfloat16 [1024, 1024], P('tp', 'dp'), may hold values from -0.75 to 0.75
- w_gate: bfloat16 [1024, 4608], P('dp', 'tp'), may hold values from -0.1875 to 0.1875
- w_up: bfloat16 [1024, 4608], P('dp', 'tp'), may hold values from -0.1875 to 0.1875
- w_down: bfloat16 [4608, 1024], P('tp', 'dp'), may hold values from -0.09375 to 0.09375
- attn_gain: bfloat16 [1024], P('dp'), may hold values from 0.25 to 1.75
- ffn_gain: bfloat16 [1024], P('dp'), may hold values from 0.25 to 1.75
- query_gain: bfloat16 [64], P('dp'), may hold values from 0.25 to 1.75
- key_gain: bfloat16 [64], P('dp'), may hold values from 0.25 to 1.75
- segment_ids: int32 [8, 1024], P('dp', 'ctx'), may hold values from 0 to 17, as said below
- valid_mask: int32 [8, 1024], P('dp', 'ctx'), may hold values from 0 to 1, as said below
- positions: int32 [8, 1024], P('dp', 'ctx'), may hold values from 0 to 2047, as said below
Outputs:
- result: float32 [8, 1024, 1024], P('dp', ('ctx', 'tp'))
- grad_hidden: float32 [8, 1024, 1024], P('dp', ('ctx', 'tp'))
- grad_w_query: float32 [1024, 1024], P('dp', 'tp')
- grad_w_key: float32 [1024, 512], P('dp', 'tp')
- grad_w_value: float32 [1024, 512], P('dp', 'tp')
- grad_w_out: float32 [1024, 1024], P('tp', 'dp')
- grad_w_gate: float32 [1024, 4608], P('dp', 'tp')
- grad_w_up: float32 [1024, 4608], P('dp', 'tp')
- grad_w_down: float32 [4608, 1024], P('tp', 'dp')
- grad_attn_gain: float32 [1024], P('dp')
- grad_ffn_gain: float32 [1024], P('dp')
- grad_query_gain: float32 [64], P('dp')
- grad_key_gain: float32 [64], P('dp')
- statistics: float32 [4], replicated
Inputs may be any that keep to these rules, and one draw needn't show every extreme that they name: `segment_ids`: within each sequence the ids never fall; its last 1 to 128 positions are padding with id 2 * 8 + 1; one document of every sequence covers positions 256 to 768. `valid_mask`: 1 exactly where segment_ids is not the padding id. Within a document consecutive tokens have consecutive positions; every sequence's first document starts at 0; the last token of every sequence has position 2047.
All inputs are finite; a program needn't handle non-finite values.
Results may differ from a plain program's by a relative error of at most 0.02.
Values may be sent and summed in bfloat16 or wider, within the bound.
A program may use at most 128 MiB of HBM per device.

v0:
```python
import jax
import jax.numpy as jnp
from jax import lax
from jax.sharding import PartitionSpec as P

EPSILON = 1e-05
ROPE_BASE = 1000000.0


def norm_rows(value):
    factor = lax.rsqrt(jnp.mean(value * value, axis=-1, keepdims=True) + EPSILON)
    return (value * factor, factor)


def norm_back(incoming, normed_hat, factor, gain):
    grad_hat = incoming * gain
    return factor * (
        grad_hat - normed_hat * jnp.mean(grad_hat * normed_hat, axis=-1, keepdims=True)
    )


def rope_tables(places, half):
    freq = ROPE_BASE ** (-(jnp.arange(half, dtype=jnp.float32) * 2.0) / (2 * half))
    angle = places.astype(jnp.float32)[:, None] * freq[None, :]
    return (jnp.cos(angle)[:, None, :], jnp.sin(angle)[:, None, :])


def rotate(value, cosine, sine, direction):
    half = value.shape[-1] // 2
    first = value[..., :half]
    second = value[..., half:]
    return jnp.concatenate(
        [first * cosine - direction * second * sine, second * cosine + direction * first * sine],
        axis=-1,
    )


def product(left, right):
    return jnp.dot(left, right, preferred_element_type=jnp.float32)


def product_tn(left, right):
    return lax.dot_general(
        left, right, (((0,), (0,)), ((), ())), preferred_element_type=jnp.float32
    )


def product_nt(left, right):
    return lax.dot_general(
        left, right, (((1,), (1,)), ((), ())), preferred_element_type=jnp.float32
    )


def per_device(
    hidden_states,
    out_grad,
    w_query,
    w_key,
    w_value,
    w_out,
    w_gate,
    w_up,
    w_down,
    attn_gain,
    ffn_gain,
    query_gain,
    key_gain,
    segment_ids,
    valid_mask,
    positions,
):
    (
        mat_query,
        mat_key,
        mat_value,
        mat_out,
        mat_gate,
        mat_up,
        mat_down,
        gain_attn,
        gain_ffn,
        gain_query,
        gain_key,
    ) = (
        lax.all_gather(w_query, "dp", axis=0, tiled=True),
        lax.all_gather(w_key, "dp", axis=0, tiled=True),
        lax.all_gather(w_value, "dp", axis=0, tiled=True),
        lax.all_gather(w_out, "dp", axis=1, tiled=True),
        lax.all_gather(w_gate, "dp", axis=0, tiled=True),
        lax.all_gather(w_up, "dp", axis=0, tiled=True),
        lax.all_gather(w_down, "dp", axis=1, tiled=True),
        lax.all_gather(attn_gain, "dp", axis=0, tiled=True),
        lax.all_gather(ffn_gain, "dp", axis=0, tiled=True),
        lax.all_gather(query_gain, "dp", axis=0, tiled=True),
        lax.all_gather(key_gain, "dp", axis=0, tiled=True),
    )
    gain_attn = gain_attn.astype(jnp.float32)
    gain_ffn = gain_ffn.astype(jnp.float32)
    gain_query = gain_query.astype(jnp.float32)
    gain_key = gain_key.astype(jnp.float32)
    seqs, local_len, width = hidden_states.shape
    rows = seqs * local_len
    head_dim = gain_query.shape[0]
    q_heads = mat_query.shape[1] // head_dim
    kv_heads = mat_key.shape[1] // head_dim
    group = q_heads // kv_heads
    scale_factor = head_dim ** (-0.5)
    share_len = local_len // lax.axis_size("tp")
    share_start = lax.axis_index("tp") * share_len

    def share_rows(value):
        shaped = value.reshape(seqs, local_len, -1)
        return lax.dynamic_slice_in_dim(shaped, share_start, share_len, 1).reshape(
            seqs * share_len, -1
        )

    hidden = hidden_states.astype(jnp.float32).reshape(rows, width)
    hidden_hat, hidden_factor = norm_rows(hidden)
    normed = (hidden_hat * gain_attn).astype(jnp.bfloat16)
    query_pre = product(normed, mat_query).reshape(rows, q_heads, head_dim)
    key_pre = product(normed, mat_key).reshape(rows, kv_heads, head_dim)
    value_low = product(normed, mat_value).astype(jnp.bfloat16)
    cosine, sine = rope_tables(positions.reshape(rows), head_dim // 2)
    query_hat, query_factor = norm_rows(query_pre)
    query_rot = rotate(query_hat * gain_query, cosine, sine, 1.0).astype(jnp.bfloat16)
    key_hat, key_factor = norm_rows(key_pre)
    key_rot = rotate(key_hat * gain_key, cosine, sine, 1.0).astype(jnp.bfloat16)
    all_keys, all_values = (
        lax.all_gather(
            key_rot.reshape(seqs, local_len, kv_heads * head_dim), "ctx", axis=1, tiled=True
        ),
        lax.all_gather(
            value_low.reshape(seqs, local_len, kv_heads * head_dim), "ctx", axis=1, tiled=True
        ),
    )
    key_segments, key_valid = (
        lax.all_gather(segment_ids, "ctx", axis=1, tiled=True),
        lax.all_gather(valid_mask, "ctx", axis=1, tiled=True),
    )
    full_len = all_keys.shape[1]
    query_index = lax.axis_index("ctx") * local_len + jnp.arange(local_len)
    key_index = jnp.arange(full_len)
    queries = query_rot.reshape(seqs, local_len, kv_heads, group, head_dim)

    def allowed_of(query_seg, key_seg, key_flag):
        same = query_seg[:, None] == key_seg[None, :]
        causal = key_index[None, :] <= query_index[:, None]
        itself = key_index[None, :] == query_index[:, None]
        return same & causal & ((key_flag[None, :] == 1) | itself)

    def masked_scores(query_blk, key_blk, query_seg, key_seg, key_flag):
        scores = (
            jnp.einsum("qhgd,khd->hgqk", query_blk, key_blk, preferred_element_type=jnp.float32)
            * scale_factor
        )
        return jnp.where(allowed_of(query_seg, key_seg, key_flag)[None, None], scores, -1e30)

    def attend(item):
        query_blk, key_flat, value_flat, query_seg, key_seg, key_flag = item
        key_blk = key_flat.reshape(full_len, kv_heads, head_dim)
        value_blk = value_flat.reshape(full_len, kv_heads, head_dim)
        scores = masked_scores(query_blk, key_blk, query_seg, key_seg, key_flag)
        highest = jnp.max(scores, axis=-1, keepdims=True)
        expo = jnp.exp(scores - highest)
        totals = jnp.sum(expo, axis=-1, keepdims=True)
        probs_low = (expo / totals).astype(jnp.bfloat16)
        output = jnp.einsum(
            "hgqk,khd->qhgd", probs_low, value_blk, preferred_element_type=jnp.float32
        )
        return (
            output.astype(jnp.bfloat16).reshape(local_len, q_heads * head_dim),
            highest[..., 0] + jnp.log(totals[..., 0]),
        )

    attn_out, log_totals = lax.map(
        attend, (queries, all_keys, all_values, segment_ids, key_segments, key_valid)
    )
    attn_out = attn_out.reshape(rows, q_heads * head_dim)
    attn_part = product(attn_out, mat_out)
    hidden_s = share_rows(hidden)
    attn = lax.psum(attn_part.astype(jnp.bfloat16), "tp").astype(jnp.float32)
    middle = hidden + attn
    middle_hat, middle_factor = norm_rows(middle)
    normed_mid = (middle_hat * gain_ffn).astype(jnp.bfloat16)
    attn_s = share_rows(attn)
    middle_s = share_rows(middle)
    mid_hat_s = share_rows(middle_hat)
    gate = product(normed_mid, mat_gate)
    upward = product(normed_mid, mat_up)
    sigmoid_gate = jax.nn.sigmoid(gate)
    inner = (gate * sigmoid_gate * upward).astype(jnp.bfloat16)
    mlp_part = product(inner, mat_down)
    mlp_s = share_rows(lax.psum(mlp_part.astype(jnp.bfloat16), "tp").astype(jnp.float32))
    result_s = middle_s + mlp_s
    keep_s = share_rows(valid_mask.reshape(rows, 1)).astype(jnp.float32)
    squares = jnp.stack(
        [
            jnp.sum(keep_s * hidden_s * hidden_s),
            jnp.sum(keep_s * attn_s * attn_s),
            jnp.sum(keep_s * middle_s * middle_s),
            jnp.sum(keep_s * mlp_s * mlp_s),
        ]
    )
    mat_query, mat_key, mat_value, mat_out, mat_gate, mat_up, mat_down = (
        lax.all_gather(w_query, "dp", axis=0, tiled=True),
        lax.all_gather(w_key, "dp", axis=0, tiled=True),
        lax.all_gather(w_value, "dp", axis=0, tiled=True),
        lax.all_gather(w_out, "dp", axis=1, tiled=True),
        lax.all_gather(w_gate, "dp", axis=0, tiled=True),
        lax.all_gather(w_up, "dp", axis=0, tiled=True),
        lax.all_gather(w_down, "dp", axis=1, tiled=True),
    )
    grad_out = out_grad.astype(jnp.float32).reshape(rows, width)
    grad_low = out_grad.reshape(rows, width)
    grad_down = product_tn(inner, grad_low)
    grad_inner = product_nt(grad_low, mat_down)
    grad_gate = (grad_inner * upward * sigmoid_gate * (1.0 + gate * (1.0 - sigmoid_gate))).astype(
        jnp.bfloat16
    )
    grad_upward = (grad_inner * gate * sigmoid_gate).astype(jnp.bfloat16)
    grad_wgate = product_tn(normed_mid, grad_gate)
    grad_wup = product_tn(normed_mid, grad_upward)
    mid_back_part = product_nt(grad_gate, mat_gate) + product_nt(grad_upward, mat_up)
    grad_normed_mid = lax.psum(mid_back_part.astype(jnp.bfloat16), "tp").astype(jnp.float32)
    grad_middle = grad_out + norm_back(grad_normed_mid, middle_hat, middle_factor, gain_ffn)
    grad_attn_low = grad_middle.astype(jnp.bfloat16)
    grad_nm_s = share_rows(grad_normed_mid)
    grad_middle_s = share_rows(grad_middle)
    ffn_part = jnp.sum(grad_nm_s * mid_hat_s, axis=0)
    grad_wout = product_tn(attn_out, grad_attn_low)
    grad_attn_out = (
        product_nt(grad_attn_low, mat_out)
        .astype(jnp.bfloat16)
        .reshape(seqs, local_len, kv_heads, group, head_dim)
    )

    def attend_back(item):
        query_blk, key_flat, value_flat, query_seg, key_seg, key_flag, log_total, grad_blk = item
        key_blk = key_flat.reshape(full_len, kv_heads, head_dim)
        value_blk = value_flat.reshape(full_len, kv_heads, head_dim)
        scores = masked_scores(query_blk, key_blk, query_seg, key_seg, key_flag)
        probs = jnp.exp(scores - log_total[..., None])
        probs_low = probs.astype(jnp.bfloat16)
        grad_value = jnp.einsum(
            "hgqk,qhgd->khd", probs_low, grad_blk, preferred_element_type=jnp.float32
        )
        grad_probs = jnp.einsum(
            "qhgd,khd->hgqk", grad_blk, value_blk, preferred_element_type=jnp.float32
        )
        row_dot = jnp.sum(probs * grad_probs, axis=-1, keepdims=True)
        grad_scores = (probs * (grad_probs - row_dot)).astype(jnp.bfloat16)
        grad_query = (
            jnp.einsum("hgqk,khd->qhgd", grad_scores, key_blk, preferred_element_type=jnp.float32)
            * scale_factor
        )
        grad_key = (
            jnp.einsum("hgqk,qhgd->khd", grad_scores, query_blk, preferred_element_type=jnp.float32)
            * scale_factor
        )
        return (
            grad_query,
            grad_key.reshape(full_len, kv_heads * head_dim),
            grad_value.reshape(full_len, kv_heads * head_dim),
        )

    grad_queries, grad_keys_all, grad_values_all = lax.map(
        attend_back,
        (
            queries,
            all_keys,
            all_values,
            segment_ids,
            key_segments,
            key_valid,
            log_totals,
            grad_attn_out,
        ),
    )
    grad_keys, grad_values = (
        lax.psum_scatter(
            grad_keys_all.astype(jnp.bfloat16), "ctx", scatter_dimension=1, tiled=True
        ).astype(jnp.float32),
        lax.psum_scatter(
            grad_values_all.astype(jnp.bfloat16), "ctx", scatter_dimension=1, tiled=True
        ).astype(jnp.float32),
    )
    grad_query_norm = rotate(grad_queries.reshape(rows, q_heads, head_dim), cosine, sine, -1.0)
    grad_key_norm = rotate(grad_keys.reshape(rows, kv_heads, head_dim), cosine, sine, -1.0)
    grad_gq_part = jnp.sum(grad_query_norm * query_hat, axis=(0, 1))
    grad_gk_part = jnp.sum(grad_key_norm * key_hat, axis=(0, 1))
    grad_query_low = (
        norm_back(grad_query_norm, query_hat, query_factor, gain_query)
        .astype(jnp.bfloat16)
        .reshape(rows, q_heads * head_dim)
    )
    grad_key_low = (
        norm_back(grad_key_norm, key_hat, key_factor, gain_key)
        .astype(jnp.bfloat16)
        .reshape(rows, kv_heads * head_dim)
    )
    grad_value_low = grad_values.astype(jnp.bfloat16).reshape(rows, kv_heads * head_dim)
    grad_wquery = product_tn(normed, grad_query_low)
    grad_wkey = product_tn(normed, grad_key_low)
    grad_wvalue = product_tn(normed, grad_value_low)
    grad_normed_part = (
        product_nt(grad_query_low, mat_query)
        + product_nt(grad_key_low, mat_key)
        + product_nt(grad_value_low, mat_value)
    )
    grad_normed_s = share_rows(
        lax.psum(grad_normed_part.astype(jnp.bfloat16), "tp").astype(jnp.float32)
    )
    hidden_hat_s = share_rows(hidden_hat)
    hidden_factor_s = share_rows(hidden_factor)
    attn_g_part = jnp.sum(grad_normed_s * hidden_hat_s, axis=0)
    grad_hidden_s = grad_middle_s + norm_back(
        grad_normed_s, hidden_hat_s, hidden_factor_s, gain_attn
    )
    square_sums, count, grad_attn_full, grad_ffn_full, grad_gq_full, grad_gk_full = lax.psum(
        (squares, jnp.sum(keep_s), attn_g_part, ffn_part, grad_gq_part, grad_gk_part),
        ("dp", "ctx", "tp"),
    )
    statistics = jnp.sqrt(square_sums / (count * width))
    width_share = attn_gain.shape[0]
    head_share = query_gain.shape[0]
    owner = lax.axis_index("dp")
    own_attn_g = lax.dynamic_slice_in_dim(grad_attn_full, owner * width_share, width_share, 0)
    own_ffn_g = lax.dynamic_slice_in_dim(grad_ffn_full, owner * width_share, width_share, 0)
    own_query_g = lax.dynamic_slice_in_dim(grad_gq_full, owner * head_share, head_share, 0)
    own_key_g = lax.dynamic_slice_in_dim(grad_gk_full, owner * head_share, head_share, 0)
    summed = (
        lax.psum(grad_wquery.astype(jnp.bfloat16), "ctx").astype(jnp.float32),
        lax.psum(grad_wkey.astype(jnp.bfloat16), "ctx").astype(jnp.float32),
        lax.psum(grad_wvalue.astype(jnp.bfloat16), "ctx").astype(jnp.float32),
        lax.psum(grad_wout.astype(jnp.bfloat16), "ctx").astype(jnp.float32),
        lax.psum(grad_wgate.astype(jnp.bfloat16), "ctx").astype(jnp.float32),
        lax.psum(grad_wup.astype(jnp.bfloat16), "ctx").astype(jnp.float32),
        lax.psum(grad_down.astype(jnp.bfloat16), "ctx").astype(jnp.float32),
    )
    owned = (
        lax.psum_scatter(
            summed[0].astype(jnp.bfloat16), "dp", scatter_dimension=0, tiled=True
        ).astype(jnp.float32),
        lax.psum_scatter(
            summed[1].astype(jnp.bfloat16), "dp", scatter_dimension=0, tiled=True
        ).astype(jnp.float32),
        lax.psum_scatter(
            summed[2].astype(jnp.bfloat16), "dp", scatter_dimension=0, tiled=True
        ).astype(jnp.float32),
        lax.psum_scatter(
            summed[3].astype(jnp.bfloat16), "dp", scatter_dimension=1, tiled=True
        ).astype(jnp.float32),
        lax.psum_scatter(
            summed[4].astype(jnp.bfloat16), "dp", scatter_dimension=0, tiled=True
        ).astype(jnp.float32),
        lax.psum_scatter(
            summed[5].astype(jnp.bfloat16), "dp", scatter_dimension=0, tiled=True
        ).astype(jnp.float32),
        lax.psum_scatter(
            summed[6].astype(jnp.bfloat16), "dp", scatter_dimension=1, tiled=True
        ).astype(jnp.float32),
    )
    return (
        result_s.reshape(seqs, share_len, width),
        grad_hidden_s.reshape(seqs, share_len, width),
        owned[0],
        owned[1],
        owned[2],
        owned[3],
        owned[4],
        owned[5],
        owned[6],
        own_attn_g,
        own_ffn_g,
        own_query_g,
        own_key_g,
        statistics,
    )


def solution(mesh):
    return jax.shard_map(
        per_device,
        mesh=mesh,
        in_specs=(
            P("dp", "ctx", None),
            P("dp", "ctx", None),
            P("dp", "tp"),
            P("dp", "tp"),
            P("dp", "tp"),
            P("tp", "dp"),
            P("dp", "tp"),
            P("dp", "tp"),
            P("tp", "dp"),
            P("dp"),
            P("dp"),
            P("dp"),
            P("dp"),
            P("dp", "ctx"),
            P("dp", "ctx"),
            P("dp", "ctx"),
        ),
        out_specs=(
            P("dp", ("ctx", "tp"), None),
            P("dp", ("ctx", "tp"), None),
            P("dp", "tp"),
            P("dp", "tp"),
            P("dp", "tp"),
            P("tp", "dp"),
            P("dp", "tp"),
            P("dp", "tp"),
            P("tp", "dp"),
            P("dp"),
            P("dp"),
            P("dp"),
            P("dp"),
            P(),
        ),
        check_vma=False,
    )
```

profile of v0, /device:TPU:0, one launch (start us, length us, event | category | flops | bytes accessed | tf_op | source)
XLA Modules:
  0.0 901.2 jit_solution(13059394335622834798)
XLA Ops:
  11.9 13.4 %all-reduce.4 = (bf16[64]{0:T(256)(128)(2,1)S(1)}, bf16[64]{0:T(256)(128)(2,1)S(1)}) all-reduce(bf16[64]{0:T(256)(128)(2,1)S(1)} %dynamic-update-slice, bf16[64]{0:T(256)(128)(2,1)S(1)} %dynamic-update-slice.1), channel_id=1, replica_groups=mesh['dp'=4,'ctx'=2,'tp'=4] {'dp'}, use_global_device_ids=true, to_apply=%add | all-reduce | flops 128 | bytes 512
  26.0 7.6 all-gather
  36.4 4.5 all_gather.56
  40.8 4.5 all_gather.55
  45.3 14.5 %all_gather.57 = bf16[1024,128]{1,0:T(8,128)(2,1)S(1)} all-gather(bf16[256,128]{1,0:T(8,128)(2,1)} %param.23), channel_id=1, replica_groups=mesh['dp'=4,'ctx'=2,'tp'=4] {'dp'}, dimensions={0}, use_global_device_ids=true | all-gather | bytes 327680 | tf_op jit(solution)/shard_map/all_gather | solution.py:86
  59.8 14.2 %all_gather.53 = bf16[1024,128]{1,0:T(8,128)(2,1)S(1)} all-gather(bf16[256,128]{1,0:T(8,128)(2,1)} %param.24), channel_id=1, replica_groups=mesh['dp'=4,'ctx'=2,'tp'=4] {'dp'}, dimensions={0}, use_global_device_ids=true | all-gather | bytes 327680 | tf_op jit(solution)/shard_map/all_gather | solution.py:87
  74.2 16.1 %all_gather.60 = bf16[1024,256]{1,0:T(8,128)(2,1)S(1)} all-gather(bf16[256,256]{1,0:T(8,128)(2,1)} %param.22), channel_id=1, replica_groups=mesh['dp'=4,'ctx'=2,'tp'=4] {'dp'}, dimensions={0}, use_global_device_ids=true | all-gather | bytes 655360 | tf_op jit(solution)/shard_map/all_gather | solution.py:85
  90.3 16.1 %all_gather.62 = bf16[256,1024]{1,0:T(8,128)(2,1)} all-gather(bf16[256,256]{1,0:T(8,128)(2,1)} %param.25), channel_id=1, replica_groups=mesh['dp'=4,'ctx'=2,'tp'=4] {'dp'}, dimensions={1}, use_global_device_ids=true | all-gather | bytes 655360 | tf_op jit(solution)/shard_map/all_gather | solution.py:88
  108.9 7.0 all_gather.54
  115.9 2.5 convert_multiply_fusion
  122.2 7.3 all_gather.59
  129.5 2.4 multiply_reduce_fusion.6
  139.5 20.9 %while.30 = (s32[]{:T(128)}, bf16[2,512,256]{2,1,0:T(8,128)(2,1)}, f32[2,2,2,512]{3,2,1,0:T(2,128)S(1)}, bf16[2,1024,128]{1,2,0:T(8,128)(2,1)S(1)}, s32[2,512]{1...) while((s32[]{:T(128)}, bf16[2,512,256]{2,1,0:T(8,128)(2,1)}, ...), condition=%wide.region_6.7_spmd.clone.clone, body=%wide.region_3.6_spmd.clone.clone.sunk | while | flops 565313024 | bytes 30503060 | solution.py:175
  140.6 2.6 fusion.147
  145.0 3.1 fusion.149
  151.1 2.6 fusion.147
  155.5 3.1 fusion.149
  160.5 3.3 convolution_convert_fusion.4
  165.6 10.4 %all-gather.1 = bf16[4,1,256]{2,1,0:T(2,128)(2,1)S(1)} all-gather(bf16[1,1,256]{2,1,0:T(2,128)(2,1)S(1)} %reshape.646), channel_id=1, replica_groups=mesh['dp'=4,'ctx'=2,'tp'=4] {'dp'}, dimensions={0}, use_global_device_ids=true | all-gather | bytes 2560 | tf_op jit(solution)/shard_map/all_gather | solution.py:93
  176.0 39.4 %all-reduce.11.cloned.1.call-done = bf16[1024,1024]{1,0:T(8,128)(2,1)} async-done(((bf16[1024,1024]{1,0:T(8,128)(2,1)}), bf16[1024,1024]{1,0:T(8,128)(2,1)}) %all-reduce.11.cloned.1.call-update) | async-done | bytes 2097168 | tf_op jit(solution)/shard_map/psum | solution.py:181
  215.3 2.5 multiply_reduce_fusion.1
  217.9 4.8 multiply_convert_fusion.3
  222.7 7.6 fusion.71
  230.2 35.9 %all-gather.6.cloned.1.call-done = bf16[1024,1152]{1,0:T(8,128)(2,1)} async-done(((bf16[256,1152]{1,0:T(8,128)(2,1)}), bf16[1024,1152]{1,0:T(8,128)(2,1)}) %all-gather.6.cloned.1.call-update) | async-done | bytes 2359312 | tf_op jit(solution)/shard_map/all_gather | solution.py:89
  266.2 7.3 fusion.70
  273.5 43.3 %all-gather.10.cloned.1.call-done = bf16[1152,1024]{1,0:T(8,128)(2,1)} async-done(((bf16[1152,256]{1,0:T(8,128)(2,1)}), bf16[1152,1024]{1,0:T(8,128)(2,1)}) %all-gather.10.cloned.1.call-update) | async-done | bytes 2359312 | tf_op jit(solution)/shard_map/all_gather | solution.py:91
  316.8 8.8 multiply_convert_fusion
  325.6 2.9 fusion.72
  329.0 4.1 add_convert_fusion.1
  333.2 49.6 %all-reduce.13.cloned.1.call-done = bf16[1024,1024]{1,0:T(8,128)(2,1)} async-done(((bf16[1024,1024]{1,0:T(8,128)(2,1)}), bf16[1024,1024]{1,0:T(8,128)(2,1)}) %all-reduce.13.cloned.1.call-update) | async-done | bytes 2097168 | tf_op jit(solution)/shard_map/psum | solution.py:224
  382.9 3.6 multiply_reduce_fusion
  387.6 2.7 multiply_add_fusion
  393.9 2.7 reshape.666
  398.9 57.5 %while.31 = (s32[]{:T(128)}, f32[2,512,2,2,64]{1,0,4,3,2:T(2,128)}, bf16[2,1024,128]{1,2,0:T(8,128)(2,1)}, bf16[2,1024,128]{2,1,0:T(8,128)(2,1)}, bf16[2,1024,12...) while((s32[]{:T(128)}, f32[2,512,2,2,64]{1,0,4,3,2:T(2,128)}, ...), condition=%wide.region_14.15_spmd.clone.clone, body=%wide.region_12.14_spmd.clone.clone.sunk | while | flops 1377172992 | bytes 133517600 | solution.py:266
  401.3 2.4 fusion.165
  405.4 5.6 fusion.161
  411.1 2.7 fusion.162
  417.3 10.4 %dynamic_update_slice.42 = f32[2,512,2,2,64]{1,0,4,3,2:T(2,128)} dynamic-update-slice(f32[2,512,2,2,64]{1,0,4,3,2:T(2,128)} %get-tuple-element.622, f32[1,512,2,2,64]{1,0,4,3,2:T(1,128)S(1)} %copy.123, s32[]{:T(128)S(6)} %copy.148, s32[]{:T(128)} %constant.59.clone.1..sunk, s32[]{:T(128)} %constant.59.clone.1..sunk, s32[]{:T(128)} %constant.59.clone.1..sunk, s32[]{:T(128)} %constant.59.clone.1..sunk) | dynamic-update-slice | bytes 1048580 | tf_op jit(solution)/shard_map/while/body/jit(dynamic_update_index_in_dim)/dynamic_update_slice | solution.py:266
  430.1 2.4 fusion.165
  434.2 5.6 fusion.161
  439.9 2.7 fusion.162
  446.0 10.4 %dynamic_update_slice.42 = f32[2,512,2,2,64]{1,0,4,3,2:T(2,128)} dynamic-update-slice(f32[2,512,2,2,64]{1,0,4,3,2:T(2,128)} %get-tuple-element.622, f32[1,512,2,2,64]{1,0,4,3,2:T(1,128)S(1)} %copy.123, s32[]{:T(128)S(6)} %copy.148, s32[]{:T(128)} %constant.59.clone.1..sunk, s32[]{:T(128)} %constant.59.clone.1..sunk, s32[]{:T(128)} %constant.59.clone.1..sunk, s32[]{:T(128)} %constant.59.clone.1..sunk) | dynamic-update-slice | bytes 1048580 | tf_op jit(solution)/shard_map/while/body/jit(dynamic_update_index_in_dim)/dynamic_update_slice | solution.py:266
  457.1 3.1 reshape.621
  460.2 4.0 convolution_convert_fusion.5
  476.7 11.3 %reduce-scatter.12.cloned.1.call-done = bf16[2,512,128]{2,1,0:T(8,128)(2,1)} async-done(((bf16[2,1024,128]{2,1,0:T(8,128)(2,1)}), bf16[2,512,128]{2,1,0:T(8,128)(2,1)}) %reduce-scatter.12.cloned.1.call-update) | async-done | bytes 262160 | tf_op jit(solution)/shard_map/reduce_scatter | solution.py:283
  488.0 2.4 fusion.55
  490.5 6.6 convolution_convert_fusion.2
  497.2 6.8 convolution_convert_fusion.1
  504.1 5.6 convolution_convert_fusion
  510.1 6.6 convolution_convert_fusion.3
  520.6 13.9 %reduce-scatter.14.cloned.1.call-done = bf16[256,256]{1,0:T(8,128)(2,1)} async-done(((bf16[1024,256]{1,0:T(8,128)(2,1)}), bf16[256,256]{1,0:T(8,128)(2,1)}) %reduce-scatter.14.cloned.1.call-update) | async-done | bytes 131088 | tf_op jit(solution)/shard_map/reduce_scatter | solution.py:341
  534.5 20.8 %reduce-scatter.16.cloned.1.call-done = bf16[256,128]{1,0:T(8,128)(2,1)} async-done(((bf16[1024,128]{1,0:T(8,128)(2,1)}), bf16[256,128]{1,0:T(8,128)(2,1)}) %reduce-scatter.16.cloned.1.call-update) | async-done | bytes 65552 | tf_op jit(solution)/shard_map/reduce_scatter | solution.py:344
  555.3 20.7 %reduce-scatter.18.cloned.1.call-done = bf16[256,128]{1,0:T(8,128)(2,1)} async-done(((bf16[1024,128]{1,0:T(8,128)(2,1)}), bf16[256,128]{1,0:T(8,128)(2,1)}) %reduce-scatter.18.cloned.1.call-update) | async-done | bytes 65552 | tf_op jit(solution)/shard_map/reduce_scatter | solution.py:347
  576.0 48.7 %reduce-scatter.22.cloned.1.call-done = bf16[256,1152]{1,0:T(8,128)(2,1)} async-done(((bf16[1024,1152]{1,0:T(8,128)(2,1)}), bf16[256,1152]{1,0:T(8,128)(2,1)}) %reduce-scatter.22.cloned.1.call-update) | async-done | bytes 589840 | tf_op jit(solution)/shard_map/reduce_scatter | solution.py:353
  624.7 49.7 %reduce-scatter.24.cloned.1.call-done = bf16[256,1152]{1,0:T(8,128)(2,1)} async-done(((bf16[1024,1152]{1,0:T(8,128)(2,1)}), bf16[256,1152]{1,0:T(8,128)(2,1)}) %reduce-scatter.24.cloned.1.call-update) | async-done | bytes 589840 | tf_op jit(solution)/shard_map/reduce_scatter | solution.py:356
  674.4 49.9 %reduce-scatter.26.cloned.1.call-done = bf16[1152,256]{1,0:T(8,128)(2,1)} async-done(((bf16[1152,1024]{1,0:T(8,128)(2,1)}), bf16[1152,256]{1,0:T(8,128)(2,1)}) %reduce-scatter.26.cloned.1.call-update) | async-done | bytes 589840 | tf_op jit(solution)/shard_map/reduce_scatter | solution.py:359
  725.6 2.4 convert_element_type.181
  728.9 4.1 bitcast_convert_fusion
  734.8 77.0 %all-reduce.15.cloned.1.call-done = (bf16[2,512,1024]{2,1,0:T(8,128)(2,1)}, bf16[2,512,1024]{2,1,0:T(8,128)(2,1)}) async-done(((bf16[2,512,1024]{2,1,0:T(8,128)(2,1)}, bf16[2,512,1024]{2,1,0:T(8,128)(2,1)}), (bf16[2,512,1024]{2,1,0:T(8,128)(2,1)}, bf16[2,512,1024]{2,1,0:T(8,128)(2,1)})) %all-reduce.15.cloned.1.call-update) | async-done | bytes 4194320 | tf_op jit(solution)/shard_map/psum | solution.py:193
  811.8 4.3 fusion.60
  816.1 2.7 pad_maximum_fusion.3
  820.3 40.0 %all-reduce.2 = (f32[1024]{0:T(1024)S(1)}, f32[1024]{0:T(1024)S(1)}, f32[64]{0:T(128)S(1)}, f32[64]{0:T(128)S(1)}, f32[4]{0:T(128)S(1)}, /*index=5*/f32[]{:T(128)}) all-reduce(f32[1024]{0:T(1024)S(1)} %get-tuple-element.308, f32[1024]{0:T(1024)S(1)} %multiply_reduce_fusion.4, ...), channel_id=1, replica_groups=mesh['dp'=4,'ctx'=2,'tp'=4] {'dp','ctx','tp'}, use_global_device_ids=true, to_apply=%region_36.37 | all-reduce | flops 2181 | bytes 17448 | tf_op jit(solution)/shard_map/psum | solution.py:319
  863.9 2.8 fusion.58
  866.7 15.0 %all-reduce.17.cloned.1.call-done = (bf16[256,256]{1,0:T(8,128)(2,1)}, bf16[256,128]{1,0:T(8,128)(2,1)}, bf16[256,128]{1,0:T(8,128)(2,1)}, bf16[256,256]{1,0:T(8...) async-done(((bf16[256,256]{1,0:T(8,128)(2,1)}, bf16[256,128]{1,0:T(8,128)(2,1)}, bf16[256,128]{1,0:T(8,128)(2,1)}, ...) | async-done | bytes 2162704 | tf_op jit(solution)/shard_map/psum | solution.py:332
  (276 shorter events, 91.8 us)
Async XLA Ops:
  8.0 99.4 %copy-start.1 = (bf16[2,512,1024]{2,1,0:T(8,128)(2,1)S(1)}, bf16[2,512,1024]{2,1,0:T(8,128)(2,1)}, u32[]{:S(2)}) copy-start(bf16[2,512,1024]{2,1,0:T(8,128)(2,1)} %param.20) | copy-start | bytes 6291460
  8.0 207.3 %all-reduce.11.cloned.1.call-start = ((), (), s32[]{:S(2)}) async-start(), calls=%async_computation.9 | async-start | bytes 4194304 | tf_op jit(solution)/shard_map/psum | solution.py:181
  25.3 96.5 %copy-start.41 = (f32[64]{0:T(128)}, f32[64]{0:T(128)S(1)}, u32[]{:S(2)}) copy-start(f32[64]{0:T(128)S(1)} %convert_element_type.187) | copy-start | bytes 772
  25.3 106.7 %copy-start.43 = (f32[64]{0:T(128)}, f32[64]{0:T(128)S(1)}, u32[]{:S(2)}) copy-start(f32[64]{0:T(128)S(1)} %convert_element_type.191) | copy-start | bytes 772
  33.6 82.4 %copy-start.38 = (f32[4,1,256]{2,1,0:T(1,128)}, f32[4,1,256]{2,1,0:T(1,128)S(1)}, u32[]{:S(2)}) copy-start(f32[4,1,256]{2,1,0:T(1,128)S(1)} %convert_element_type.229) | copy-start | bytes 12292
  36.3 79.6 %copy-start.40 = (f32[2,512]{1,0:T(2,128)}, f32[2,512]{1,0:T(2,128)S(1)}, u32[]{:S(2)}) copy-start(f32[2,512]{1,0:T(2,128)S(1)} %get-tuple-element.411) | copy-start | bytes 12292
  59.8 14.3 %copy-start.23 = (bf16[1024,128]{1,0:T(8,128)(2,1)}, bf16[1024,128]{1,0:T(8,128)(2,1)S(1)}, u32[]{:S(2)}) copy-start(bf16[1024,128]{1,0:T(8,128)(2,1)S(1)} %all_gather.57) | copy-start | bytes 786436
  74.1 34.6 %copy-start.21 = (bf16[1024,128]{1,0:T(8,128)(2,1)}, bf16[1024,128]{1,0:T(8,128)(2,1)S(1)}, u32[]{:S(2)}) copy-start(bf16[1024,128]{1,0:T(8,128)(2,1)S(1)} %all_gather.53) | copy-start | bytes 786436
  90.3 18.4 %copy-start.14 = (bf16[1024,256]{1,0:T(8,128)(2,1)}, bf16[1024,256]{1,0:T(8,128)(2,1)S(1)}, u32[]{:S(2)}) copy-start(bf16[1024,256]{1,0:T(8,128)(2,1)S(1)} %all_gather.60) | copy-start | bytes 1572868
  121.8 11.4 %copy-start.19 = (f32[1024,32]{0,1:T(8,128)}, f32[1024,32]{0,1:T(8,128)S(1)}, u32[]{:S(2)}) copy-start(f32[1024,32]{0,1:T(8,128)S(1)} %get-tuple-element.410) | copy-start | bytes 393220
  131.9 7.6 copy-start.35
  132.0 2.1 copy-start.33
  160.5 5.1 copy-start.47
  163.8 58.9 %all-gather.8.cloned.1.call-start = ((), (), s32[]{:S(2)}) async-start(), calls=%async_computation.11 | async-start | bytes 2949120 | tf_op jit(solution)/shard_map/all_gather | solution.py:90
  164.4 101.8 %all-gather.6.cloned.1.call-start = ((), (), s32[]{:S(2)}) async-start(), calls=%async_computation.10 | async-start | bytes 2949120 | tf_op jit(solution)/shard_map/all_gather | solution.py:89
  165.0 151.8 %all-gather.10.cloned.1.call-start = ((), (), s32[]{:S(2)}) async-start(), calls=%async_computation.12 | async-start | bytes 2949120 | tf_op jit(solution)/shard_map/all_gather | solution.py:91
  165.5 217.3 %all-reduce.13.cloned.1.call-start = ((), (), s32[]{:S(2)}) async-start(), calls=%async_computation.13 | async-start | bytes 4194304 | tf_op jit(solution)/shard_map/psum | solution.py:224
  215.3 2.5 copy-start.7
  230.2 86.5 %copy-start.25 = (bf16[2,512,1024]{2,1,0:T(8,128)(2,1)S(1)}, bf16[2,512,1024]{2,1,0:T(8,128)(2,1)}, u32[]{:S(2)}) copy-start(bf16[2,512,1024]{2,1,0:T(8,128)(2,1)} %param.21) | copy-start | bytes 6291460
  316.8 8.8 copy-start.46
  325.6 2.9 copy-start.48
  325.6 2.9 copy-start.49
  325.6 3.4 copy-start.45
  333.1 138.1 %reduce-scatter.10.cloned.1.call-start = ((), (), s32[]{:S(2)}) async-start(), calls=%async_computation.14 | async-start | bytes 786432 | tf_op jit(solution)/shard_map/reduce_scatter | solution.py:280
  382.9 4.1 copy-start.3
  382.9 4.7 copy-start.8
  387.6 4.7 copy-start.18
  390.3 2.0 copy-start.4
  392.3 6.6 copy-start.10
  401.3 3.2 copy-start
  404.7 6.4 slice-start
  405.4 5.7 slice-start.1
  430.1 3.2 copy-start
  433.4 6.4 slice-start
  434.2 5.7 slice-start.1
  456.4 31.6 %reduce-scatter.12.cloned.1.call-start = ((), (), s32[]{:S(2)}) async-start(), calls=%async_computation.15 | async-start | bytes 786432 | tf_op jit(solution)/shard_map/reduce_scatter | solution.py:283
  456.5 8.0 copy-start.20
  456.5 8.0 copy-start.29
  457.0 63.5 %reduce-scatter.20.cloned.1.call-start = ((), (), s32[]{:S(2)}) async-start(), calls=%async_computation.19 | async-start | bytes 655360 | tf_op jit(solution)/shard_map/reduce_scatter | solution.py:350
  460.2 5.8 copy-start.12
  460.2 5.8 copy-start.34
  460.2 5.9 copy-start.44
  464.2 3.4 copy-start.6
  464.2 70.3 %reduce-scatter.14.cloned.1.call-start = ((), (), s32[]{:S(2)}) async-start(), calls=%async_computation.16 | async-start | bytes 655360 | tf_op jit(solution)/shard_map/reduce_scatter | solution.py:341
  467.6 7.2 copy-start.17
  467.6 7.2 copy-start.37
  467.6 7.2 copy-start.42
  469.2 86.1 %reduce-scatter.16.cloned.1.call-start = ((), (), s32[]{:S(2)}) async-start(), calls=%async_computation.17 | async-start | bytes 327680 | tf_op jit(solution)/shard_map/reduce_scatter | solution.py:344
  476.7 99.4 %reduce-scatter.18.cloned.1.call-start = ((), (), s32[]{:S(2)}) async-start(), calls=%async_computation.18 | async-start | bytes 327680 | tf_op jit(solution)/shard_map/reduce_scatter | solution.py:347
  490.4 134.3 %reduce-scatter.22.cloned.1.call-start = ((), (), s32[]{:S(2)}) async-start(), calls=%async_computation.20 | async-start | bytes 2949120 | tf_op jit(solution)/shard_map/reduce_scatter | solution.py:353
  497.2 6.9 copy-start.26
  497.2 177.3 %reduce-scatter.24.cloned.1.call-start = ((), (), s32[]{:S(2)}) async-start(), calls=%async_computation.21 | async-start | bytes 2949120 | tf_op jit(solution)/shard_map/reduce_scatter | solution.py:356
  504.0 220.3 %reduce-scatter.26.cloned.1.call-start = ((), (), s32[]{:S(2)}) async-start(), calls=%async_computation.22 | async-start | bytes 2949120 | tf_op jit(solution)/shard_map/reduce_scatter | solution.py:359
  509.8 6.9 copy-start.15
  509.8 6.9 copy-start.28
  509.8 302.1 %all-reduce.15.cloned.1.call-start = ((), (), s32[]{:S(2)}) async-start(), calls=%async_computation.23 | async-start | bytes 8388608 | tf_op jit(solution)/shard_map/psum | solution.py:193
  516.7 1.7 copy-start.22
  516.7 1.7 copy-start.30
  520.4 205.2 %copy-start.2 = (bf16[2,512,1024]{2,1,0:T(8,128)(2,1)S(1)}, bf16[2,512,1024]{2,1,0:T(8,128)(2,1)}, u32[]{:S(2)}) copy-start(bf16[2,512,1024]{2,1,0:T(8,128)(2,1)} %param.20) | copy-start | bytes 6291460
  520.5 361.2 %all-reduce.17.cloned.1.call-start = ((), (), s32[]{:S(2)}) async-start(), calls=%async_computation.24 | async-start | bytes 4325376 | tf_op jit(solution)/shard_map/psum | solution.py:332
  728.1 4.9 copy-start.9
  733.4 85.3 %copy-start.39 = (f32[4,1,256]{2,1,0:T(1,128)S(1)}, f32[4,1,256]{2,1,0:T(1,128)}, u32[]{:S(2)}) copy-start(f32[4,1,256]{2,1,0:T(1,128)} %copy-done.38) | copy-start | bytes 12292
  811.8 7.0 copy-start.32
  881.7 10.6 %copy-start.31 = (bf16[1152,256]{1,0:T(8,128)(2,1)S(1)}, bf16[1152,256]{1,0:T(8,128)(2,1)}, u32[]{:S(2)}) copy-start(bf16[1152,256]{1,0:T(8,128)(2,1)} %get-tuple-element.380) | copy-start | bytes 1769476
  (8 other events, 9.3 us)
Sparse Core Ops, SparseCore 0:
  163.9 51.3 all-reduce.10
  333.3 49.5 all-reduce.12
  456.6 14.6 reduce-scatter.9
  473.4 14.5 reduce-scatter.11
  490.1 21.6 reduce-scatter.19
  514.5 19.9 reduce-scatter.13
  537.3 17.9 reduce-scatter.15
  558.2 17.7 reduce-scatter.17
  578.3 46.3 reduce-scatter.21
  626.9 47.5 reduce-scatter.23
  676.8 47.5 reduce-scatter.25
  726.6 85.1 all-reduce.14
  814.8 66.8 all-reduce.16
Sparse Core Ops, SparseCore 1:
  165.9 50.0 all-gather.7
  217.5 48.6 all-gather.5
  267.7 49.0 all-gather.9
where the time goes:
time: 908 us; the launch traced here: 901 us
  waiting for transfers between devices  480 us (53%)
  blocking collectives  156 us (17%)
  matrix products  113 us (12%)
  other arithmetic  71.9 us (8%)
  local copies, waits for them, and re-layouts  61.9 us (7%)
  between operations  18 us (2%)
    psum x1, waiting for transfers between devices, per_device(): lax.psum(mlp_part.astype(jnp.bfloat16), 'tp').astype(jnp.float32)  77 us
    reduce_scatter x1, waiting for transfers between devices, per_device(): lax.psum_scatter(summed[6].astype(jnp.bfloat16), 'dp', scatter_dimension=...  49.9 us
    reduce_scatter x1, waiting for transfers between devices, per_device(): lax.psum_scatter(summed[5].astype(jnp.bfloat16), 'dp', scatter_dimension=...  49.7 us
    psum x1, waiting for transfers between devices, per_device(): lax.psum(mid_back_part.astype(jnp.bfloat16), 'tp').astype(jnp.float32)  49.6 us
    reduce_scatter x1, waiting for transfers between devices, per_device(): lax.psum_scatter(summed[4].astype(jnp.bfloat16), 'dp', scatter_dimension=...  48.7 us
    all_gather x1, waiting for transfers between devices, per_device(): lax.all_gather(w_down, 'dp', axis=1, tiled=True)  43.3 us
    psum x1, blocking collectives, per_device(): lax.psum((squares, jnp.sum(keep_s), attn_g_part, ffn_part, grad_gq_part,...  40 us
    psum x1, waiting for transfers between devices, per_device(): attn = lax.psum(attn_part.astype(jnp.bfloat16), 'tp').astype(jnp.float32)  39.4 us
  transfers between devices with their start and end apart: 16, of which 14 were waited for; matrix products, arithmetic and copies ran while one was open for 11% of the time, Pallas kernels for 0%

commit v1 on v0

v1 whole, which is shorter than its diff:
```python
import jax
import jax.numpy as jnp
from jax import lax
from jax.sharding import PartitionSpec as P

EPSILON = 1e-05
ROPE_BASE = 1000000.0
F32 = jnp.float32
BF16 = jnp.bfloat16


def norm_rows(value):
    factor = lax.rsqrt(jnp.mean(value * value, axis=-1, keepdims=True) + EPSILON)
    return (value * factor, factor)


def norm_back(incoming, normed_hat, factor, gain):
    grad_hat = incoming * gain
    return factor * (
        grad_hat - normed_hat * jnp.mean(grad_hat * normed_hat, axis=-1, keepdims=True)
    )


def rope_tables(places, half):
    freq = ROPE_BASE ** (-(jnp.arange(half, dtype=F32) * 2.0) / (2 * half))
    angle = places.astype(F32)[:, None] * freq[None, :]
    return (jnp.cos(angle)[:, None, :], jnp.sin(angle)[:, None, :])


def rotate(value, cosine, sine, direction):
    half = value.shape[-1] // 2
    first = value[..., :half]
    second = value[..., half:]
    return jnp.concatenate(
        [first * cosine - direction * second * sine, second * cosine + direction * first * sine],
        axis=-1,
    )


def product(left, right):
    return jnp.dot(left, right, preferred_element_type=F32)


def product_tn(left, right):
    return lax.dot_general(left, right, (((0,), (0,)), ((), ())), preferred_element_type=F32)


def product_nt(left, right):
    return lax.dot_general(left, right, (((1,), (1,)), ((), ())), preferred_element_type=F32)


def shift_send(value, axis, step):
    size = lax.axis_size(axis)
    return lax.ppermute(value, axis, [(i, (i + step) % size) for i in range(size)])


def put(buffer, piece, *starts):
    return lax.dynamic_update_slice(buffer, piece, tuple(starts) + (0,) * (buffer.ndim - len(starts)))


def take(value, index, axis):
    return lax.dynamic_index_in_dim(value, index, axis, keepdims=False)


def gather_weight(shard):
    parts, halves = lax.axis_size("dp"), lax.axis_size("ctx")
    me, side = lax.axis_index("dp"), lax.axis_index("ctx")
    rows, width = shard.shape
    split = shard.reshape(halves, rows // halves, width)
    mine = take(split, side, 0)
    whole = jnp.zeros((parts, halves, rows // halves, width), shard.dtype)
    whole = put(whole, split[None], me)
    for step in range(1, parts):
        piece = shift_send(mine, "dp", step)
        owner = (me - step) % parts
        whole = put(whole, piece[None, None], owner, side)
        for turn in range(1, halves):
            other = shift_send(piece, "ctx", turn)
            whole = put(whole, other[None, None], owner, (side - turn) % halves)
    return whole.reshape(parts * rows, width)


def scatter_weight(grad):
    parts, halves = lax.axis_size("dp"), lax.axis_size("ctx")
    me, side = lax.axis_index("dp"), lax.axis_index("ctx")
    rows, width = grad.shape
    rows = rows // (parts * halves)
    low = grad.astype(BF16).reshape(parts, halves, rows, width)
    total = take(low, side, 1).astype(F32)
    for turn in range(1, halves):
        total += shift_send(take(low, (side + turn) % halves, 1), "ctx", turn).astype(F32)
    low = total.astype(BF16)
    mine = take(low, me, 0).astype(F32)
    for step in range(1, parts):
        mine += shift_send(take(low, (me + step) % parts, 0), "dp", step).astype(F32)
    mine = mine.astype(BF16)
    whole = jnp.zeros((halves, rows, width), BF16)
    whole = put(whole, mine[None], side)
    for turn in range(1, halves):
        whole = put(whole, shift_send(mine, "ctx", turn)[None], (side - turn) % halves)
    return whole.reshape(halves * rows, width).astype(F32)


def tp_pairs(size):
    return [(i, i ^ 1) for i in range(size)]


def tp_chip(size, step):
    return [(i, (i + 2 * step) % size) for i in range(size)]


def tp_scatter(value):
    size, me = lax.axis_size("tp"), lax.axis_index("tp")
    seqs, tokens, width = value.shape
    core, chip, chips = me % 2, me // 2, size // 2
    low = value.astype(BF16).reshape(seqs, chips, 2, tokens // size, width)
    total = take(low, core, 2).astype(F32) + lax.ppermute(
        take(low, 1 - core, 2), "tp", tp_pairs(size)
    ).astype(F32)
    low = total.astype(BF16)
    mine = take(low, chip, 1).astype(F32)
    for step in range(1, chips):
        piece = take(low, (chip + step) % chips, 1)
        mine += lax.ppermute(piece, "tp", tp_chip(size, step)).astype(F32)
    return mine


def tp_gather(value):
    size, me = lax.axis_size("tp"), lax.axis_index("tp")
    seqs, share, width = value.shape
    core, chip, chips = me % 2, me // 2, size // 2
    whole = jnp.zeros((seqs, chips, 2, share, width), value.dtype)
    pair = jnp.zeros((seqs, chips, share, width), value.dtype)
    pair = put(pair, value[:, None], 0, chip)
    for step in range(1, chips):
        piece = lax.ppermute(value, "tp", tp_chip(size, step))
        pair = put(pair, piece[:, None], 0, (chip - step) % chips)
    other = lax.ppermute(pair, "tp", tp_pairs(size))
    whole = put(whole, pair[:, :, None], 0, 0, core)
    whole = put(whole, other[:, :, None], 0, 0, 1 - core)
    return whole.reshape(seqs, size * share, width)


def tiles_of(width):
    return 3 if width % 3 == 0 else 1


def per_device(
    hidden_states,
    out_grad,
    w_query,
    w_key,
    w_value,
    w_out,
    w_gate,
    w_up,
    w_down,
    attn_gain,
    ffn_gain,
    query_gain,
    key_gain,
    segment_ids,
    valid_mask,
    positions,
):
    seqs, local_len, width = hidden_states.shape
    rows = seqs * local_len
    share_len = local_len // lax.axis_size("tp")
    share_start = lax.axis_index("tp") * share_len
    nq, nk = w_query.shape[1], w_key.shape[1]
    hidden_units = w_gate.shape[1]
    tiles = tiles_of(hidden_units)
    tile = hidden_units // tiles

    gains = lax.all_gather(
        jnp.concatenate([attn_gain, ffn_gain, query_gain, key_gain]), "dp", axis=0
    ).astype(F32)
    marks = []
    start = 0
    for gain in (attn_gain, ffn_gain, query_gain, key_gain):
        marks.append(gains[:, start : start + gain.shape[0]].reshape(-1))
        start += gain.shape[0]
    gain_attn, gain_ffn, gain_query, gain_key = marks

    mat_attn = gather_weight(jnp.concatenate([w_query, w_key, w_value, w_out.T], axis=1))
    mat_ffn = []
    for i in range(tiles):
        cut = slice(i * tile, (i + 1) * tile)
        mat_ffn.append(
            gather_weight(jnp.concatenate([w_gate[:, cut], w_up[:, cut], w_down[cut].T], axis=1))
        )
    mat_qkv, mat_out_t = mat_attn[:, : nq + 2 * nk], mat_attn[:, nq + 2 * nk :]

    head_dim = gain_query.shape[0]
    q_heads, kv_heads = nq // head_dim, nk // head_dim
    group = q_heads // kv_heads
    scale_factor = head_dim ** (-0.5)

    def share_rows(value):
        return lax.dynamic_slice_in_dim(value, share_start, share_len, 1)

    hidden = hidden_states.astype(F32).reshape(rows, width)
    hidden_hat, hidden_factor = norm_rows(hidden)
    normed = (hidden_hat * gain_attn).astype(BF16)
    qkv = product(normed, mat_qkv)
    query_pre = qkv[:, :nq].reshape(rows, q_heads, head_dim)
    key_pre = qkv[:, nq : nq + nk].reshape(rows, kv_heads, head_dim)
    value_low = qkv[:, nq + nk :].astype(BF16)
    cosine, sine = rope_tables(positions.reshape(rows), head_dim // 2)
    query_hat, query_factor = norm_rows(query_pre)
    query_rot = rotate(query_hat * gain_query, cosine, sine, 1.0).astype(BF16)
    key_hat, key_factor = norm_rows(key_pre)
    key_rot = rotate(key_hat * gain_key, cosine, sine, 1.0).astype(BF16)
    halves, side = lax.axis_size("ctx"), lax.axis_index("ctx")
    full_len = halves * local_len

    def ctx_gather(value):
        whole = jnp.zeros((seqs, halves) + value.shape[1:], value.dtype)
        whole = put(whole, value[:, None], 0, side)
        for turn in range(1, halves):
            whole = put(whole, shift_send(value, "ctx", turn)[:, None], 0, (side - turn) % halves)
        return whole.reshape((seqs, full_len) + value.shape[2:])

    kv_low = jnp.concatenate([key_rot.reshape(rows, nk), value_low], axis=1)
    all_kv = ctx_gather(kv_low.reshape(seqs, local_len, 2 * nk))
    all_keys, all_values = all_kv[..., :nk], all_kv[..., nk:]
    key_facts = ctx_gather(jnp.stack([segment_ids, valid_mask], axis=-1))
    key_segments, key_valid = key_facts[..., 0], key_facts[..., 1]
    query_index = side * local_len + jnp.arange(local_len)
    key_index = jnp.arange(full_len)
    queries = query_rot.reshape(seqs, local_len, kv_heads, group, head_dim)

    def allowed_of(query_seg, key_seg, key_flag):
        same = query_seg[:, None] == key_seg[None, :]
        causal = key_index[None, :] <= query_index[:, None]
        itself = key_index[None, :] == query_index[:, None]
        return same & causal & ((key_flag[None, :] == 1) | itself)

    def masked_scores(query_blk, key_blk, query_seg, key_seg, key_flag):
        scores = (
            jnp.einsum("qhgd,khd->hgqk", query_blk, key_blk, preferred_element_type=F32)
            * scale_factor
        )
        return jnp.where(allowed_of(query_seg, key_seg, key_flag)[None, None], scores, -1e30)

    def attend(item):
        query_blk, key_flat, value_flat, query_seg, key_seg, key_flag = item
        key_blk = key_flat.reshape(full_len, kv_heads, head_dim)
        value_blk = value_flat.reshape(full_len, kv_heads, head_dim)
        scores = masked_scores(query_blk, key_blk, query_seg, key_seg, key_flag)
        highest = jnp.max(scores, axis=-1, keepdims=True)
        expo = jnp.exp(scores - highest)
        totals = jnp.sum(expo, axis=-1, keepdims=True)
        probs_low = (expo / totals).astype(BF16)
        output = jnp.einsum("hgqk,khd->qhgd", probs_low, value_blk, preferred_element_type=F32)
        return (
            output.astype(BF16).reshape(local_len, q_heads * head_dim),
            highest[..., 0] + jnp.log(totals[..., 0]),
        )

    attn_out, log_totals = lax.map(
        attend, (queries, all_keys, all_values, segment_ids, key_segments, key_valid)
    )
    attn_out = attn_out.reshape(rows, q_heads * head_dim)
    attn_part = product_nt(attn_out, mat_out_t).reshape(seqs, local_len, width)
    attn_s = tp_scatter(attn_part)
    hidden_s = share_rows(hidden_states).astype(F32)
    middle_s = hidden_s + attn_s
    mid_hat_s, mid_factor_s = norm_rows(middle_s)
    normed_mid = tp_gather((mid_hat_s * gain_ffn).astype(BF16)).reshape(rows, width)

    grad_low = out_grad.reshape(rows, width)
    mlp_part = jnp.zeros((rows, width), F32)
    back_part = jnp.zeros((rows, width), F32)
    ffn_grads = []
    for mat in mat_ffn:
        both, mat_down_t = mat[:, : 2 * tile], mat[:, 2 * tile :]
        pre = product(normed_mid, both)
        gate, upward = pre[:, :tile], pre[:, tile:]
        sigmoid_gate = jax.nn.sigmoid(gate)
        inner = (gate * sigmoid_gate * upward).astype(BF16)
        grad_inner = product(grad_low, mat_down_t)
        grad_gate = (
            grad_inner * upward * sigmoid_gate * (1.0 + gate * (1.0 - sigmoid_gate))
        ).astype(BF16)
        grad_upward = (grad_inner * gate * sigmoid_gate).astype(BF16)
        mlp_part += product_nt(inner, mat_down_t)
        grad_both = jnp.concatenate([grad_gate, grad_upward], axis=1)
        back_part += product_nt(grad_both, both)
        ffn_grads.append(
            scatter_weight(
                jnp.concatenate(
                    [product_tn(normed_mid, grad_both), product_tn(grad_low, inner)], axis=1
                )
            )
        )
    grad_nm_s = tp_scatter(back_part.reshape(seqs, local_len, width))
    grad_out_s = share_rows(out_grad).astype(F32)
    grad_middle_s = grad_out_s + norm_back(grad_nm_s, mid_hat_s, mid_factor_s, gain_ffn)
    grad_attn_low = tp_gather(grad_middle_s.astype(BF16)).reshape(rows, width)
    ffn_part = jnp.sum(grad_nm_s * mid_hat_s, axis=(0, 1))
    mlp_s = tp_scatter(mlp_part.reshape(seqs, local_len, width))
    result_s = middle_s + mlp_s
    keep_s = share_rows(valid_mask[..., None]).astype(F32)
    squares = jnp.stack(
        [
            jnp.sum(keep_s * hidden_s * hidden_s),
            jnp.sum(keep_s * attn_s * attn_s),
            jnp.sum(keep_s * middle_s * middle_s),
            jnp.sum(keep_s * mlp_s * mlp_s),
        ]
    )
    grad_wout_t = product_tn(grad_attn_low, attn_out)
    grad_attn_out = (
        product(grad_attn_low, mat_out_t)
        .astype(BF16)
        .reshape(seqs, local_len, kv_heads, group, head_dim)
    )

    def attend_back(item):
        query_blk, key_flat, value_flat, query_seg, key_seg, key_flag, log_total, grad_blk = item
        key_blk = key_flat.reshape(full_len, kv_heads, head_dim)
        value_blk = value_flat.reshape(full_len, kv_heads, head_dim)
        scores = masked_scores(query_blk, key_blk, query_seg, key_seg, key_flag)
        probs = jnp.exp(scores - log_total[..., None])
        probs_low = probs.astype(BF16)
        grad_value = jnp.einsum(
            "hgqk,qhgd->khd", probs_low, grad_blk, preferred_element_type=F32
        )
        grad_probs = jnp.einsum(
            "qhgd,khd->hgqk", grad_blk, value_blk, preferred_element_type=F32
        )
        row_dot = jnp.sum(probs * grad_probs, axis=-1, keepdims=True)
        grad_scores = (probs * (grad_probs - row_dot)).astype(BF16)
        grad_query = (
            jnp.einsum("hgqk,khd->qhgd", grad_scores, key_blk, preferred_element_type=F32)
            * scale_factor
        )
        grad_key = (
            jnp.einsum("hgqk,qhgd->khd", grad_scores, query_blk, preferred_element_type=F32)
            * scale_factor
        )
        return (
            grad_query,
            grad_key.reshape(full_len, kv_heads * head_dim),
            grad_value.reshape(full_len, kv_heads * head_dim),
        )

    grad_queries, grad_keys_all, grad_values_all = lax.map(
        attend_back,
        (
            queries,
            all_keys,
            all_values,
            segment_ids,
            key_segments,
            key_valid,
            log_totals,
            grad_attn_out,
        ),
    )
    grad_kv_all = (
        jnp.concatenate([grad_keys_all, grad_values_all], axis=-1)
        .astype(BF16)
        .reshape(seqs, halves, local_len, 2 * nk)
    )
    grad_kv = take(grad_kv_all, side, 1).astype(F32)
    for turn in range(1, halves):
        piece = take(grad_kv_all, (side + turn) % halves, 1)
        grad_kv += shift_send(piece, "ctx", turn).astype(F32)
    grad_keys, grad_values = grad_kv[..., :nk], grad_kv[..., nk:]
    grad_query_norm = rotate(grad_queries.reshape(rows, q_heads, head_dim), cosine, sine, -1.0)
    grad_key_norm = rotate(grad_keys.reshape(rows, kv_heads, head_dim), cosine, sine, -1.0)
    grad_gq_part = jnp.sum(grad_query_norm * query_hat, axis=(0, 1))
    grad_gk_part = jnp.sum(grad_key_norm * key_hat, axis=(0, 1))
    grad_query_low = (
        norm_back(grad_query_norm, query_hat, query_factor, gain_query)
        .astype(BF16)
        .reshape(rows, nq)
    )
    grad_key_low = (
        norm_back(grad_key_norm, key_hat, key_factor, gain_key).astype(BF16).reshape(rows, nk)
    )
    grad_value_low = grad_values.astype(BF16).reshape(rows, nk)
    grad_qkv = jnp.concatenate([grad_query_low, grad_key_low, grad_value_low], axis=1)
    attn_grads = scatter_weight(
        jnp.concatenate([product_tn(normed, grad_qkv), grad_wout_t], axis=1)
    )
    grad_normed_s = tp_scatter(product_nt(grad_qkv, mat_qkv).reshape(seqs, local_len, width))
    hidden_hat_s, hidden_factor_s = norm_rows(hidden_s)
    attn_g_part = jnp.sum(grad_normed_s * hidden_hat_s, axis=(0, 1))
    grad_hidden_s = grad_middle_s + norm_back(
        grad_normed_s, hidden_hat_s, hidden_factor_s, gain_attn
    )
    packed = jnp.concatenate(
        [
            attn_g_part,
            ffn_part,
            grad_gq_part,
            grad_gk_part,
            squares,
            jnp.sum(keep_s)[None],
        ]
    )
    packed = lax.psum(packed, ("dp", "ctx", "tp"))
    grad_attn_full, grad_ffn_full = packed[:width], packed[width : 2 * width]
    rest = packed[2 * width :]
    grad_gq_full, grad_gk_full = rest[:head_dim], rest[head_dim : 2 * head_dim]
    square_sums, count = rest[2 * head_dim : 2 * head_dim + 4], rest[2 * head_dim + 4]
    statistics = jnp.sqrt(square_sums / (count * width))
    owner = lax.axis_index("dp")

    def own(value, like):
        size = like.shape[0]
        return lax.dynamic_slice_in_dim(value, owner * size, size, 0)

    return (
        result_s,
        grad_hidden_s,
        attn_grads[:, :nq],
        attn_grads[:, nq : nq + nk],
        attn_grads[:, nq + nk : nq + 2 * nk],
        attn_grads[:, nq + 2 * nk :].T,
        jnp.concatenate([g[:, :tile] for g in ffn_grads], axis=1),
        jnp.concatenate([g[:, tile : 2 * tile] for g in ffn_grads], axis=1),
        jnp.concatenate([g[:, 2 * tile :].T for g in ffn_grads], axis=0),
        own(grad_attn_full, attn_gain),
        own(grad_ffn_full, ffn_gain),
        own(grad_gq_full, query_gain),
        own(grad_gk_full, key_gain),
        statistics,
    )


def solution(mesh):
    return jax.shard_map(
        per_device,
        mesh=mesh,
        in_specs=(
            P("dp", "ctx", None),
            P("dp", "ctx", None),
            P("dp", "tp"),
            P("dp", "tp"),
            P("dp", "tp"),
            P("tp", "dp"),
            P("dp", "tp"),
            P("dp", "tp"),
            P("tp", "dp"),
            P("dp"),
            P("dp"),
            P("dp"),
            P("dp"),
            P("dp", "ctx"),
            P("dp", "ctx"),
            P("dp", "ctx"),
        ),
        out_specs=(
            P("dp", ("ctx", "tp"), None),
            P("dp", ("ctx", "tp"), None),
            P("dp", "tp"),
            P("dp", "tp"),
            P("dp", "tp"),
            P("tp", "dp"),
            P("dp", "tp"),
            P("dp", "tp"),
            P("tp", "dp"),
            P("dp"),
            P("dp"),
            P("dp"),
            P("dp"),
            P(),
        ),
        check_vma=False,
    )
```

time: 908 us -> 768 us (0.85)
  waiting for transfers between devices: 480 us -> 189 us
  local copies, waits for them, and re-layouts: 61.9 us -> 243 us
  blocking collectives: 156 us -> 48.6 us
  starting transfers between devices: 1.12 us -> 91.5 us
  between operations: 18 us -> 4.07 us
    reduce_scatter x9 -> x0, waiting for transfers between devices: 217 us -> none  [the longest x1 49.9 us: per_device(): lax.psum_scatter(summed[6].astype(jnp.bfloat16), 'dp', scatter_dimension=...]
    ppermute x0 -> x59, waiting for transfers between devices: none -> 189 us  [the longest x47 178 us: shift_send(): lax.ppermute(value, axis, [(i, (i + step) % size) for i in range(size)])]
    psum x4 -> x0, waiting for transfers between devices: 181 us -> none  [the longest x1 77 us: per_device(): lax.psum(mlp_part.astype(jnp.bfloat16), 'tp').astype(jnp.float32)]
    all_gather x10 -> x0, blocking collectives: 102 us -> none  [the longest x1 16.1 us: per_device(): lax.all_gather(w_out, 'dp', axis=1, tiled=True)]
    ppermute x0 -> x59, starting transfers between devices: none -> 91.5 us  [the longest x47 83.8 us: shift_send(): lax.ppermute(value, axis, [(i, (i + step) % size) for i in range(size)])]
    dynamic_update_slice x0 -> x43, local copies, waits for them, and re-layouts: none -> 82.7 us  [put(): lax.dynamic_update_slice(buffer, piece, tuple(starts) + (0,) * (buffer.nd...]
    all_gather x3 -> x0, waiting for transfers between devices: 79.2 us -> none  [the longest x1 43.3 us: per_device(): lax.all_gather(w_down, 'dp', axis=1, tiled=True)]
    unnamed x107 -> x277, local copies, waits for them, and re-layouts: 14.6 us -> 41.6 us
  transfers between devices with their start and end apart: 16 -> 59, of which waited for: 14 -> 23; matrix products, arithmetic and copies ran while one was open for 11% -> 32% of each run, Pallas kernels for 0% -> 0%
where the time goes in v1:
time: 768 us; the launch traced here: 756 us
  local copies, waits for them, and re-layouts  243 us (32%)
  waiting for transfers between devices  189 us (25%)
  matrix products  106 us (14%)
  starting transfers between devices  91.5 us (12%)
  other arithmetic  73.2 us (10%)
  blocking collectives  48.6 us (6%)
    ppermute x47, waiting for transfers between devices, shift_send(): lax.ppermute(value, axis, [(i, (i + step) % size) for i in range(size)])  178 us
    ppermute x47, starting transfers between devices, shift_send(): lax.ppermute(value, axis, [(i, (i + step) % size) for i in range(size)])  83.8 us
    dynamic_update_slice x43, local copies, waits for them, and re-layouts, put(): lax.dynamic_update_slice(buffer, piece, tuple(starts) + (0,) * (buffer.nd...  82.7 us
    unnamed x277, local copies, waits for them, and re-layouts  41.6 us
    psum x1, blocking collectives, per_device(): packed = lax.psum(packed, ('dp', 'ctx', 'tp'))  37.2 us
    dot_general x8, matrix products, product_nt(): lax.dot_general(left, right, (((1,), (1,)), ((), ())), preferred_element_...  29 us
    dot_general x8, matrix products, product(): return jnp.dot(left, right, preferred_element_type=F32)  27.3 us
    dynamic_update_slice x6, local copies, waits for them, and re-layouts, per_device(): lax.map(attend_back, (queries, all_keys, all_values, segment_ids, key_seg...  25.3 us
  transfers between devices with their start and end apart: 59, of which 23 were waited for; matrix products, arithmetic and copies ran while one was open for 32% of the time, Pallas kernels for 0%

profile of v1, /device:TPU:0, one launch (start us, length us, event | category | flops | bytes accessed | tf_op | source)
XLA Modules:
  0.0 755.9 jit_solution(17814261736216536450)
XLA Ops:
  6.1 5.0 collective-permute-start.4
  20.4 2.8 collective-permute-start.28
  25.3 11.4 %all-reduce = bf16[2176]{0:T(1024)(128)(2,1)S(1)} all-reduce(bf16[2176]{0:T(1024)(128)(2,1)S(1)} %dynamic-update-slice), channel_id=2, replica_groups=mesh['dp'=4,'ctx'=2,'tp'=4] {'dp'}, use_global_device_ids=true, to_apply=%add | all-reduce | flops 2176 | bytes 8704
  75.4 3.0 collective-permute-start.26
  80.0 5.3 collective-permute-done.18
  85.3 3.8 collective-permute-start.12
  90.7 4.8 collective-permute-done.12
  95.5 4.7 collective-permute-start.24
  100.9 4.2 collective-permute-done.24
  108.3 3.7 collective-permute-start.16
  115.4 5.1 collective-permute-start.14
  123.4 4.5 collective-permute-done.5
  145.0 9.4 %dynamic_update_slice.170 = bf16[2,2,512,256]{2,1,3,0:T(2,128)(2,1)S(1)} dynamic-update-slice(bf16[2,2,512,256]{2,1,3,0:T(2,128)(2,1)S(1)} %broadcast_in_dim.226, bf16[2,1,512,256]{2,1,3,0:T(2,128)(2,1)S(1)} %copy.273, s32[]{:T(128)} %constant.399.clone.1, s32[]{:T(128)S(6)} %select_n.331, s32[]{:T(128)} %constant.399.clone.1, s32[]{:T(128)} %constant.399.clone.1) | dynamic-update-slice | bytes 1048580 | tf_op jit(solution)/shard_map/dynamic_update_slice | solution.py:58
  156.0 4.6 collective-permute-start.20
  162.3 6.4 collective-permute-done.20
  171.5 7.4 collective-permute-done.13
  185.0 3.5 collective-permute-done.15
  192.0 3.6 collective-permute-done.6
  197.0 9.4 %dynamic_update_slice.171 = bf16[2,2,512,256]{2,1,3,0:T(2,128)(2,1)S(1)} dynamic-update-slice(bf16[2,2,512,256]{2,1,3,0:T(2,128)(2,1)S(1)} %dynamic_update_slice.170, bf16[2,1,512,256]{2,1,3,0:T(2,128)(2,1)S(1)} %copy.275, s32[]{:T(128)} %constant.399.clone.1, s32[]{:T(128)S(6)} %select_n.335, s32[]{:T(128)} %constant.399.clone.1, s32[]{:T(128)} %constant.399.clone.1) | dynamic-update-slice | bytes 1048580 | tf_op jit(solution)/shard_map/dynamic_update_slice | solution.py:58
  207.3 14.6 %while.30 = (s32[]{:T(128)}, bf16[2,512,256]{1,2,0:T(8,128)(2,1)S(1)}, f32[2,2,2,512]{3,2,1,0:T(2,128)S(1)}, bf16[2,1024,128]{1,2,0:T(8,128)(2,1)S(1)}, s32[2,51...) while((s32[]{:T(128)}, ...), condition=%wide.region_6.7_spmd.clone.clone, body=%wide.region_3.6_spmd.clone.clone.sunk | while | flops 565313024 | bytes 29978772 | solution.py:261
  236.0 18.3 %collective-permute-done.27 = bf16[128,1152]{1,0:T(8,128)(2,1)S(1)} collective-permute-done((bf16[128,1152]{1,0:T(8,128)(2,1)}, bf16[128,1152]{1,0:T(8,128)(2,1)S(1)}, u32[]{:S(2)}, u32[]{:S(2)}) %collective-permute-start.27) | collective-permute-done | bytes 294944 | tf_op jit(solution)/shard_map/ppermute | solution.py:54
  262.7 9.6 %collective-permute-done.10 = bf16[2,128,1024]{2,1,0:T(8,128)(2,1)S(1)} collective-permute-done((bf16[2,128,1024]{2,1,0:T(8,128)(2,1)S(1)}, bf16[2,128,1024]{2,1,0:T(8,128)(2,1)S(1)}, u32[]{:S(2)}, u32[]{:S(2)}) %collective-permute-start.10) | collective-permute-done | bytes 524320 | tf_op jit(solution)/shard_map/ppermute | solution.py:136
  278.6 4.1 fusion.91
  282.7 3.7 fusion.76
  288.3 4.5 fusion.138
  292.8 4.1 copy.372
  296.9 4.1 fusion.87
  301.0 3.8 fusion.71
  304.7 5.5 fusion.89
  310.2 3.0 convolution_convert_fusion.4
  313.2 3.0 convolution_convert_fusion.3
  316.2 5.5 fusion.85
  321.7 3.3 fusion.83
  325.0 4.2 fusion.66
  333.5 2.8 fusion.134
  339.8 3.9 add_convert_fusion
  373.8 9.0 %collective-permute-done.54 = bf16[4,128,1152]{2,1,0:T(8,128)(2,1)} collective-permute-done((bf16[4,128,1152]{2,1,0:T(8,128)(2,1)}, bf16[4,128,1152]{2,1,0:T(8,128)(2,1)}, u32[]{:S(2)}, u32[]{:S(2)}) %collective-permute-start.54) | collective-permute-done | bytes 1179680 | tf_op jit(solution)/shard_map/ppermute | solution.py:54
  384.8 23.1 %collective-permute-done.49 = bf16[4,128,1152]{2,1,0:T(8,128)(2,1)S(1)} collective-permute-done((bf16[4,128,1152]{2,1,0:T(8,128)(2,1)}, bf16[4,128,1152]{2,1,0:T(8,128)(2,1)S(1)}, u32[]{:S(2)}, u32[]{:S(2)}) %collective-permute-start.49) | collective-permute-done | bytes 1179680 | tf_op jit(solution)/shard_map/ppermute | solution.py:54
  407.9 3.1 collective-permute-start.57
  411.4 21.4 %collective-permute-done.44 = bf16[4,128,1152]{2,1,0:T(8,128)(2,1)S(1)} collective-permute-done((bf16[4,128,1152]{2,1,0:T(8,128)(2,1)S(1)}, bf16[4,128,1152]{2,1,0:T(8,128)(2,1)S(1)}, u32[]{:S(2)}, u32[]{:S(2)}) %collective-permute-start.44) | collective-permute-done | bytes 1179680 | tf_op jit(solution)/shard_map/ppermute | solution.py:54
  433.3 3.3 collective-permute-start.50
  437.2 19.0 %collective-permute-done.56 = bf16[128,1152]{1,0:T(8,128)(2,1)S(1)} collective-permute-done((bf16[128,1152]{1,0:T(8,128)(2,1)S(1)}, bf16[128,1152]{1,0:T(8,128)(2,1)S(1)}, u32[]{:S(2)}, u32[]{:S(2)}) %collective-permute-start.56) | collective-permute-done | bytes 294944 | tf_op jit(solution)/shard_map/ppermute | solution.py:54
  457.1 9.0 %collective-permute-start.45 = (bf16[128,1152]{1,0:T(8,128)(2,1)S(1)}, bf16[128,1152]{1,0:T(8,128)(2,1)S(1)}, u32[]{:S(2)}, u32[]{:S(2)}) collective-permute-start(bf16[128,1152]{1,0:T(8,128)(2,1)S(1)} %get-tuple-element.523), channel_id=1, source_target_pairs={{0,8},{8,16},{16,24},{24,0},{1,9},{9,17},{17,25},{25,1},{2,10},{10... | collective-permute-start | bytes 884744 | tf_op jit(solution)/shard_map/ppermute | solution.py:54
  466.1 14.4 %collective-permute-done.51 = bf16[128,1152]{1,0:T(8,128)(2,1)S(1)} collective-permute-done((bf16[128,1152]{1,0:T(8,128)(2,1)S(1)}, bf16[128,1152]{1,0:T(8,128)(2,1)S(1)}, u32[]{:S(2)}, u32[]{:S(2)}) %collective-permute-start.51) | collective-permute-done | bytes 294944 | tf_op jit(solution)/shard_map/ppermute | solution.py:54
  483.1 3.5 collective-permute-done.47
  488.1 11.2 %collective-permute-done.46 = bf16[128,1152]{1,0:T(8,128)(2,1)S(1)} collective-permute-done((bf16[128,1152]{1,0:T(8,128)(2,1)S(1)}, bf16[128,1152]{1,0:T(8,128)(2,1)S(1)}, u32[]{:S(2)}, u32[]{:S(2)}) %collective-permute-start.46) | collective-permute-done | bytes 294944 | tf_op jit(solution)/shard_map/ppermute | solution.py:54
  504.8 4.8 fusion.115
  518.9 14.6 %dynamic_update_slice.206 = bf16[2,128,1152]{1,0,2:T(2,128)(2,1)S(1)} dynamic-update-slice(bf16[2,128,1152]{1,0,2:T(2,128)(2,1)S(1)} %copy.330, bf16[1,128,1152]{1,0,2:T(2,128)(2,1)} %copy.331, s32[]{:T(128)S(6)} %select_n.335, s32[]{:T(128)} %constant.399.clone.1, s32[]{:T(128)} %constant.399.clone.1) | dynamic-update-slice | bytes 589828 | tf_op jit(solution)/shard_map/dynamic_update_slice | solution.py:58
  544.5 3.5 copy.307
  548.0 55.9 %while.31 = (s32[]{:T(128)}, f32[2,512,2,2,64]{1,0,4,3,2:T(2,128)}, bf16[2,1024,128]{1,2,0:T(8,128)(2,1)}, bf16[2,1024,128]{1,2,0:T(8,128)(2,1)}, bf16[2,1024,12...) while((s32[]{:T(128)}, f32[2,512,2,2,64]{1,0,4,3,2:T(2,128)}, ...), condition=%wide.region_12.13_spmd.clone.clone, body=%wide.region_10.12_spmd.clone.clone.sunk | while | flops 1377172992 | bytes 72175808 | solution.py:349
  550.6 4.0 fusion.256
  554.6 3.8 fusion.253
  563.9 10.3 %dynamic_update_slice.274 = f32[2,512,2,2,64]{1,0,4,3,2:T(2,128)} dynamic-update-slice(f32[2,512,2,2,64]{1,0,4,3,2:T(2,128)} %get-tuple-element.785, f32[1,512,2,2,64]{1,0,4,3,2:T(1,128)S(1)} %copy.444, s32[]{:T(128)S(6)} %copy.504, s32[]{:T(128)} %constant.399.clone.1..sunk, s32[]{:T(128)} %constant.399.clone.1..sunk, s32[]{:T(128)} %constant.399.clone.1..sunk, s32[]{:T(128)} %constant.399.clone.1..sunk) | dynamic-update-slice | bytes 1048580 | tf_op jit(solution)/shard_map/while/body/jit(dynamic_update_index_in_dim)/dynamic_update_slice | solution.py:349
  578.4 4.0 fusion.256
  582.4 3.8 fusion.253
  591.6 10.3 %dynamic_update_slice.274 = f32[2,512,2,2,64]{1,0,4,3,2:T(2,128)} dynamic-update-slice(f32[2,512,2,2,64]{1,0,4,3,2:T(2,128)} %get-tuple-element.785, f32[1,512,2,2,64]{1,0,4,3,2:T(1,128)S(1)} %copy.444, s32[]{:T(128)S(6)} %copy.504, s32[]{:T(128)} %constant.399.clone.1..sunk, s32[]{:T(128)} %constant.399.clone.1..sunk, s32[]{:T(128)} %constant.399.clone.1..sunk, s32[]{:T(128)} %constant.399.clone.1..sunk) | dynamic-update-slice | bytes 1048580 | tf_op jit(solution)/shard_map/while/body/jit(dynamic_update_index_in_dim)/dynamic_update_slice | solution.py:349
  620.1 3.3 convolution_convert_fusion.9
  661.6 3.8 collective-permute-start.42
  665.5 5.7 collective-permute-done.40
  673.2 6.6 collective-permute-done.41
  690.9 9.5 %dynamic_update_slice.204 = bf16[2,128,768]{1,0,2:T(2,128)(2,1)S(1)} dynamic-update-slice(bf16[2,128,768]{1,0,2:T(2,128)(2,1)S(1)} %copy.325, bf16[1,128,768]{1,0,2:T(2,128)(2,1)S(1)} %copy.326, s32[]{:T(128)S(6)} %select_n.335, s32[]{:T(128)} %constant.399.clone.1, s32[]{:T(128)} %constant.399.clone.1) | dynamic-update-slice | bytes 393220 | tf_op jit(solution)/shard_map/dynamic_update_slice | solution.py:58
  707.4 3.4 concatenate.141
  710.8 37.2 %psum.7 = f32[2181]{0:T(1024)S(1)} all-reduce(f32[2181]{0:T(1024)S(1)} %concatenate.141), channel_id=1, replica_groups=mesh['dp'=4,'ctx'=2,'tp'=4] {'dp','ctx','tp'}, use_global_device_ids=true, to_apply=%region_27.28 | all-reduce | flops 2181 | bytes 17448 | tf_op jit(solution)/shard_map/psum | solution.py:405
  752.3 3.4 fusion.111
  (646 shorter events, 316.1 us)
Async XLA Ops:
  6.1 109.3 %collective-permute-start.4 = (bf16[128,768]{1,0:T(8,128)(2,1)}, bf16[128,768]{1,0:T(8,128)(2,1)}, u32[]{:S(2)}, u32[]{:S(2)}) collective-permute-start(bf16[128,768]{1,0:T(8,128)(2,1)} %bitcast.4), channel_id=1, source_target_pairs={{0,24},{8,0},{16,8},{24,16},{1,25},{9,1},{17,9},{25,17},{2,26},{10... | collective-permute-start | bytes 589832 | tf_op jit(solution)/shard_map/ppermute | solution.py:54
  11.2 97.2 %collective-permute-start.2 = (bf16[128,768]{1,0:T(8,128)(2,1)}, bf16[128,768]{1,0:T(8,128)(2,1)}, u32[]{:S(2)}, u32[]{:S(2)}) collective-permute-start(bf16[128,768]{1,0:T(8,128)(2,1)} %bitcast.4), channel_id=1, source_target_pairs={{0,16},{8,24},{16,0},{24,8},{1,17},{9,25},{17,1},{25,9},{2,18},{10... | collective-permute-start | bytes 589832 | tf_op jit(solution)/shard_map/ppermute | solution.py:54
  11.2 64.2 %collective-permute-start = (bf16[128,768]{1,0:T(8,128)(2,1)}, bf16[128,768]{1,0:T(8,128)(2,1)}, u32[]{:S(2)}, u32[]{:S(2)}) collective-permute-start(bf16[128,768]{1,0:T(8,128)(2,1)} %bitcast.4), channel_id=1, source_target_pairs={{0,8},{8,16},{16,24},{24,0},{1,9},{9,17},{17,25},{25,1},{2,10},{10... | collective-permute-start | bytes 589832 | tf_op jit(solution)/shard_map/ppermute | solution.py:54
  12.8 60.0 %collective-permute-start.7 = (s32[2,512,2]{1,0,2:T(2,128)}, s32[2,512,2]{1,0,2:T(2,128)}, u32[]{:S(2)}, u32[]{:S(2)}) collective-permute-start(s32[2,512,2]{1,0,2:T(2,128)} %get-tuple-element.571), channel_id=1, source_target_pairs={{0,4},{4,0},{1,5},{5,1},{2,6},{6,2},{3,7},{7,3},{8,12},{12,8},{9,1... | collective-permute-start | bytes 24584 | tf_op jit(solution)/shard_map/ppermute | solution.py:54
  20.4 207.6 %collective-permute-start.28 = (bf16[128,1152]{1,0:T(8,128)(2,1)}, bf16[128,1152]{1,0:T(8,128)(2,1)}, u32[]{:S(2)}, u32[]{:S(2)}) collective-permute-start(bf16[128,1152]{1,0:T(8,128)(2,1)} %dynamic-slice_bitcast_fusion.15), channel_id=1, source_target_pairs={{0,24},{8,0},{16,8},{24,16},{1,25},{9,1},{17,9},{25,17},{2,26},{10... | collective-permute-start | bytes 884744 | tf_op jit(solution)/shard_map/ppermute | solution.py:54
  55.6 81.6 %copy-start.35 = (f32[1024,32]{0,1:T(8,128)}, f32[1024,32]{0,1:T(8,128)S(1)}, u32[]{:S(2)}) copy-start(f32[1024,32]{0,1:T(8,128)S(1)} %get-tuple-element.575) | copy-start | bytes 393220
  68.8 66.0 %copy-start.106 = (f32[64]{0:T(128)}, f32[64]{0:T(128)S(1)}, u32[]{:S(2)}) copy-start(f32[64]{0:T(128)S(1)} %mul.558) | copy-start | bytes 772
  72.8 12.5 %collective-permute-start.18 = (bf16[128,1152]{1,0:T(8,128)(2,1)}, bf16[128,1152]{1,0:T(8,128)(2,1)}, u32[]{:S(2)}, u32[]{:S(2)}) collective-permute-start(bf16[128,1152]{1,0:T(8,128)(2,1)} %dynamic-slice_bitcast_fusion.16), channel_id=1, source_target_pairs={{0,8},{8,16},{16,24},{24,0},{1,9},{9,17},{17,25},{25,1},{2,10},{10... | collective-permute-start | bytes 884744 | tf_op jit(solution)/shard_map/ppermute | solution.py:54
  75.4 153.1 %collective-permute-start.26 = (bf16[128,1152]{1,0:T(8,128)(2,1)}, bf16[128,1152]{1,0:T(8,128)(2,1)}, u32[]{:S(2)}, u32[]{:S(2)}) collective-permute-start(bf16[128,1152]{1,0:T(8,128)(2,1)} %dynamic-slice_bitcast_fusion.15), channel_id=1, source_target_pairs={{0,16},{8,24},{16,0},{24,8},{1,17},{9,25},{17,1},{25,9},{2,18},{10... | collective-permute-start | bytes 884744 | tf_op jit(solution)/shard_map/ppermute | solution.py:54
  85.3 10.2 %collective-permute-start.12 = (bf16[128,1152]{1,0:T(8,128)(2,1)}, bf16[128,1152]{1,0:T(8,128)(2,1)S(1)}, u32[]{:S(2)}, u32[]{:S(2)}) collective-permute-start(bf16[128,1152]{1,0:T(8,128)(2,1)} %dynamic-slice_bitcast_fusion.17), channel_id=1, source_target_pairs={{0,8},{8,16},{16,24},{24,0},{1,9},{9,17},{17,25},{25,1},{2,10},{10... | collective-permute-start | bytes 884744 | tf_op jit(solution)/shard_map/ppermute | solution.py:54
  95.5 9.6 %collective-permute-start.24 = (bf16[128,1152]{1,0:T(8,128)(2,1)}, bf16[128,1152]{1,0:T(8,128)(2,1)}, u32[]{:S(2)}, u32[]{:S(2)}) collective-permute-start(bf16[128,1152]{1,0:T(8,128)(2,1)} %dynamic-slice_bitcast_fusion.15), channel_id=1, source_target_pairs={{0,8},{8,16},{16,24},{24,0},{1,9},{9,17},{17,25},{25,1},{2,10},{10... | collective-permute-start | bytes 884744 | tf_op jit(solution)/shard_map/ppermute | solution.py:54
  105.1 7.0 collective-permute-start.1
  108.3 115.7 %collective-permute-start.16 = (bf16[128,1152]{1,0:T(8,128)(2,1)}, bf16[128,1152]{1,0:T(8,128)(2,1)}, u32[]{:S(2)}, u32[]{:S(2)}) collective-permute-start(bf16[128,1152]{1,0:T(8,128)(2,1)} %dynamic-slice_bitcast_fusion.17), channel_id=1, source_target_pairs={{0,24},{8,0},{16,8},{24,16},{1,25},{9,1},{17,9},{25,17},{2,26},{10... | collective-permute-start | bytes 884744 | tf_op jit(solution)/shard_map/ppermute | solution.py:54
  112.0 8.5 %collective-permute-start.3 = (bf16[128,768]{1,0:T(8,128)(2,1)}, bf16[128,768]{1,0:T(8,128)(2,1)S(1)}, u32[]{:S(2)}, u32[]{:S(2)}) collective-permute-start(bf16[128,768]{1,0:T(8,128)(2,1)} %collective-permute-done.2), channel_id=1, source_target_pairs={{0,4},{4,0},{1,5},{5,1},{2,6},{6,2},{3,7},{7,3},{8,12},{12,8},{9,1... | collective-permute-start | bytes 589832 | tf_op jit(solution)/shard_map/ppermute | solution.py:54
  115.4 54.6 %collective-permute-start.14 = (bf16[128,1152]{1,0:T(8,128)(2,1)}, bf16[128,1152]{1,0:T(8,128)(2,1)}, u32[]{:S(2)}, u32[]{:S(2)}) collective-permute-start(bf16[128,1152]{1,0:T(8,128)(2,1)} %dynamic-slice_bitcast_fusion.17), channel_id=1, source_target_pairs={{0,16},{8,24},{16,0},{24,8},{1,17},{9,25},{17,1},{25,9},{2,18},{10... | collective-permute-start | bytes 884744 | tf_op jit(solution)/shard_map/ppermute | solution.py:54
  120.5 7.4 collective-permute-start.5
  127.9 28.1 %collective-permute-start.19 = (bf16[128,1152]{1,0:T(8,128)(2,1)}, bf16[128,1152]{1,0:T(8,128)(2,1)}, u32[]{:S(2)}, u32[]{:S(2)}) collective-permute-start(bf16[128,1152]{1,0:T(8,128)(2,1)} %collective-permute-done.18), channel_id=1, source_target_pairs={{0,4},{4,0},{1,5},{5,1},{2,6},{6,2},{3,7},{7,3},{8,12},{12,8},{9,1... | collective-permute-start | bytes 884744 | tf_op jit(solution)/shard_map/ppermute | solution.py:54
  156.0 12.7 %collective-permute-start.20 = (bf16[128,1152]{1,0:T(8,128)(2,1)}, bf16[128,1152]{1,0:T(8,128)(2,1)S(1)}, u32[]{:S(2)}, u32[]{:S(2)}) collective-permute-start(bf16[128,1152]{1,0:T(8,128)(2,1)} %dynamic-slice_bitcast_fusion.16), channel_id=1, source_target_pairs={{0,16},{8,24},{16,0},{24,8},{1,17},{9,25},{17,1},{25,9},{2,18},{10... | collective-permute-start | bytes 884744 | tf_op jit(solution)/shard_map/ppermute | solution.py:54
  168.7 10.2 %collective-permute-start.13 = (bf16[128,1152]{1,0:T(8,128)(2,1)}, bf16[128,1152]{1,0:T(8,128)(2,1)S(1)}, u32[]{:S(2)}, u32[]{:S(2)}) collective-permute-start(bf16[128,1152]{1,0:T(8,128)(2,1)} %copy-done.81), channel_id=1, source_target_pairs={{0,4},{4,0},{1,5},{5,1},{2,6},{6,2},{3,7},{7,3},{8,12},{12,8},{9,1... | collective-permute-start | bytes 884744 | tf_op jit(solution)/shard_map/ppermute | solution.py:54
  169.9 13.7 %collective-permute-start.21 = (bf16[128,1152]{1,0:T(8,128)(2,1)S(1)}, bf16[128,1152]{1,0:T(8,128)(2,1)S(1)}, u32[]{:S(2)}, u32[]{:S(2)}) collective-permute-start(bf16[128,1152]{1,0:T(8,128)(2,1)S(1)} %collective-permute-done.20), channel_id=1, source_target_pairs={{0,4},{4,0},{1,5},{5,1},{2,6},{6,2},{3,7},{7,3},{8,12},{12,8},{9,1... | collective-permute-start | bytes 884744 | tf_op jit(solution)/shard_map/ppermute | solution.py:54
  178.8 9.7 %collective-permute-start.15 = (bf16[128,1152]{1,0:T(8,128)(2,1)}, bf16[128,1152]{1,0:T(8,128)(2,1)S(1)}, u32[]{:S(2)}, u32[]{:S(2)}) collective-permute-start(bf16[128,1152]{1,0:T(8,128)(2,1)} %collective-permute-done.14), channel_id=1, source_target_pairs={{0,4},{4,0},{1,5},{5,1},{2,6},{6,2},{3,7},{7,3},{8,12},{12,8},{9,1... | collective-permute-start | bytes 884744 | tf_op jit(solution)/shard_map/ppermute | solution.py:54
  183.7 11.9 %collective-permute-start.6 = (bf16[2,512,256]{1,0,2:T(2,128)(2,1)S(1)}, bf16[2,512,256]{1,0,2:T(2,128)(2,1)S(1)}, u32[]{:S(2)}, u32[]{:S(2)}) collective-permute-start(bf16[2,512,256]{1,0,2:T(2,128)(2,1)S(1)} %pad_maximum_fusion.18), channel_id=1, source_target_pairs={{0,4},{4,0},{1,5},{5,1},{2,6},{6,2},{3,7},{7,3},{8,12},{12,8},{9,1... | collective-permute-start | bytes 1572872 | tf_op jit(solution)/shard_map/ppermute | solution.py:54
  188.5 37.3 %collective-permute-start.22 = (bf16[128,1152]{1,0:T(8,128)(2,1)}, bf16[128,1152]{1,0:T(8,128)(2,1)S(1)}, u32[]{:S(2)}, u32[]{:S(2)}) collective-permute-start(bf16[128,1152]{1,0:T(8,128)(2,1)} %dynamic-slice_bitcast_fusion.16), channel_id=1, source_target_pairs={{0,24},{8,0},{16,8},{24,16},{1,25},{9,1},{17,9},{25,17},{2,26},{10... | collective-permute-start | bytes 884744 | tf_op jit(solution)/shard_map/ppermute | solution.py:54
  195.6 34.4 %collective-permute-start.25 = (bf16[128,1152]{1,0:T(8,128)(2,1)}, bf16[128,1152]{1,0:T(8,128)(2,1)}, u32[]{:S(2)}, u32[]{:S(2)}) collective-permute-start(bf16[128,1152]{1,0:T(8,128)(2,1)} %collective-permute-done.24), channel_id=1, source_target_pairs={{0,4},{4,0},{1,5},{5,1},{2,6},{6,2},{3,7},{7,3},{8,12},{12,8},{9,1... | collective-permute-start | bytes 884744 | tf_op jit(solution)/shard_map/ppermute | solution.py:54
  224.0 8.3 %collective-permute-start.8 = (bf16[2,2,128,1024]{3,2,0,1:T(8,128)(2,1)S(1)}, bf16[2,2,128,1024]{3,2,0,1:T(8,128)(2,1)S(1)}, u32[]{:S(2)}, u32[]{:S(2)}) collective-permute-start(bf16[2,2,128,1024]{3,2,0,1:T(8,128)(2,1)S(1)} %bitcast.687), channel_id=1, source_target_pairs={{0,1},{1,0},{2,3},{3,2},{4,5},{5,4},{6,7},{7,6},{8,9},{9,8},{10,11... | collective-permute-start | bytes 3145736 | tf_op jit(solution)/shard_map/ppermute | solution.py:117
  225.8 47.4 %collective-permute-start.17 = (bf16[128,1152]{1,0:T(8,128)(2,1)}, bf16[128,1152]{1,0:T(8,128)(2,1)S(1)}, u32[]{:S(2)}, u32[]{:S(2)}) collective-permute-start(bf16[128,1152]{1,0:T(8,128)(2,1)} %collective-permute-done.16), channel_id=1, source_target_pairs={{0,4},{4,0},{1,5},{5,1},{2,6},{6,2},{3,7},{7,3},{8,12},{12,8},{9,1... | collective-permute-start | bytes 884744 | tf_op jit(solution)/shard_map/ppermute | solution.py:54
  228.0 34.0 %collective-permute-start.23 = (bf16[128,1152]{1,0:T(8,128)(2,1)S(1)}, bf16[128,1152]{1,0:T(8,128)(2,1)S(1)}, u32[]{:S(2)}, u32[]{:S(2)}) collective-permute-start(bf16[128,1152]{1,0:T(8,128)(2,1)S(1)} %collective-permute-done.22), channel_id=1, source_target_pairs={{0,4},{4,0},{1,5},{5,1},{2,6},{6,2},{3,7},{7,3},{8,12},{12,8},{9,1... | collective-permute-start | bytes 884744 | tf_op jit(solution)/shard_map/ppermute | solution.py:54
  228.6 45.3 %collective-permute-start.29 = (bf16[128,1152]{1,0:T(8,128)(2,1)}, bf16[128,1152]{1,0:T(8,128)(2,1)S(1)}, u32[]{:S(2)}, u32[]{:S(2)}) collective-permute-start(bf16[128,1152]{1,0:T(8,128)(2,1)} %collective-permute-done.28), channel_id=1, source_target_pairs={{0,4},{4,0},{1,5},{5,1},{2,6},{6,2},{3,7},{7,3},{8,12},{12,8},{9,1... | collective-permute-start | bytes 884744 | tf_op jit(solution)/shard_map/ppermute | solution.py:54
  230.0 24.3 %collective-permute-start.27 = (bf16[128,1152]{1,0:T(8,128)(2,1)}, bf16[128,1152]{1,0:T(8,128)(2,1)S(1)}, u32[]{:S(2)}, u32[]{:S(2)}) collective-permute-start(bf16[128,1152]{1,0:T(8,128)(2,1)} %collective-permute-done.26), channel_id=1, source_target_pairs={{0,4},{4,0},{1,5},{5,1},{2,6},{6,2},{3,7},{7,3},{8,12},{12,8},{9,1... | collective-permute-start | bytes 884744 | tf_op jit(solution)/shard_map/ppermute | solution.py:54
  232.8 22.4 %collective-permute-start.9 = (bf16[2,128,1024]{2,1,0:T(8,128)(2,1)S(1)}, bf16[2,128,1024]{2,1,0:T(8,128)(2,1)S(1)}, u32[]{:S(2)}, u32[]{:S(2)}) collective-permute-start(bf16[2,128,1024]{2,1,0:T(8,128)(2,1)S(1)} %dynamic-slice_bitcast_fusion.5), channel_id=1, source_target_pairs={{0,2},{1,3},{2,0},{3,1},{4,6},{5,7},{6,4},{7,5},{8,10},{9,11},{10,... | collective-permute-start | bytes 1572872 | tf_op jit(solution)/shard_map/ppermute | solution.py:124
  258.8 13.5 %collective-permute-start.10 = (bf16[2,128,1024]{2,1,0:T(8,128)(2,1)S(1)}, bf16[2,128,1024]{2,1,0:T(8,128)(2,1)S(1)}, u32[]{:S(2)}, u32[]{:S(2)}) collective-permute-start(bf16[2,128,1024]{2,1,0:T(8,128)(2,1)S(1)} %get-tuple-element.477), channel_id=1, source_target_pairs={{0,2},{1,3},{2,0},{3,1},{4,6},{5,7},{6,4},{7,5},{8,10},{9,11},{10,... | collective-permute-start | bytes 1572872 | tf_op jit(solution)/shard_map/ppermute | solution.py:136
  273.1 4.1 collective-permute-start.11
  350.2 15.3 %collective-permute-start.30 = (bf16[2,2,128,1024]{3,2,0,1:T(8,128)(2,1)}, bf16[2,2,128,1024]{3,2,0,1:T(8,128)(2,1)}, u32[]{:S(2)}, u32[]{:S(2)}) collective-permute-start(bf16[2,2,128,1024]{3,2,0,1:T(8,128)(2,1)} %bitcast.562), channel_id=1, source_target_pairs={{0,1},{1,0},{2,3},{3,2},{4,5},{5,4},{6,7},{7,6},{8,9},{9,8},{10,11... | collective-permute-start | bytes 3145736 | tf_op jit(solution)/shard_map/ppermute | solution.py:117
  350.7 18.9 %collective-permute-start.32 = (bf16[2,2,128,1024]{3,2,0,1:T(8,128)(2,1)}, bf16[2,2,128,1024]{3,2,0,1:T(8,128)(2,1)}, u32[]{:S(2)}, u32[]{:S(2)}) collective-permute-start(bf16[2,2,128,1024]{3,2,0,1:T(8,128)(2,1)} %bitcast.561), channel_id=1, source_target_pairs={{0,1},{1,0},{2,3},{3,2},{4,5},{5,4},{6,7},{7,6},{8,9},{9,8},{10,11... | collective-permute-start | bytes 3145736 | tf_op jit(solution)/shard_map/ppermute | solution.py:117
  353.7 29.1 %collective-permute-start.54 = (bf16[4,128,1152]{2,1,0:T(8,128)(2,1)}, bf16[4,128,1152]{2,1,0:T(8,128)(2,1)}, u32[]{:S(2)}, u32[]{:S(2)}) collective-permute-start(bf16[4,128,1152]{2,1,0:T(8,128)(2,1)} %fusion.97), channel_id=1, source_target_pairs={{0,4},{4,0},{1,5},{5,1},{2,6},{6,2},{3,7},{7,3},{8,12},{12,8},{9,1... | collective-permute-start | bytes 3538952 | tf_op jit(solution)/shard_map/ppermute | solution.py:54
  362.1 45.9 %collective-permute-start.49 = (bf16[4,128,1152]{2,1,0:T(8,128)(2,1)}, bf16[4,128,1152]{2,1,0:T(8,128)(2,1)S(1)}, u32[]{:S(2)}, u32[]{:S(2)}) collective-permute-start(bf16[4,128,1152]{2,1,0:T(8,128)(2,1)} %fusion.101), channel_id=1, source_target_pairs={{0,4},{4,0},{1,5},{5,1},{2,6},{6,2},{3,7},{7,3},{8,12},{12,8},{9,1... | collective-permute-start | bytes 3538952 | tf_op jit(solution)/shard_map/ppermute | solution.py:54
  364.0 68.8 %collective-permute-start.44 = (bf16[4,128,1152]{2,1,0:T(8,128)(2,1)S(1)}, bf16[4,128,1152]{2,1,0:T(8,128)(2,1)S(1)}, u32[]{:S(2)}, u32[]{:S(2)}) collective-permute-start(bf16[4,128,1152]{2,1,0:T(8,128)(2,1)S(1)} %fusion.105), channel_id=1, source_target_pairs={{0,4},{4,0},{1,5},{5,1},{2,6},{6,2},{3,7},{7,3},{8,12},{12,8},{9,1... | collective-permute-start | bytes 3538952 | tf_op jit(solution)/shard_map/ppermute | solution.py:54
  368.1 136.7 %collective-permute-start.31 = (bf16[2,128,1024]{2,1,0:T(8,128)(2,1)}, bf16[2,128,1024]{2,1,0:T(8,128)(2,1)}, u32[]{:S(2)}, u32[]{:S(2)}) collective-permute-start(bf16[2,128,1024]{2,1,0:T(8,128)(2,1)} %dynamic-slice_bitcast_fusion.4), channel_id=1, source_target_pairs={{0,2},{1,3},{2,0},{3,1},{4,6},{5,7},{6,4},{7,5},{8,10},{9,11},{10,... | collective-permute-start | bytes 1572872 | tf_op jit(solution)/shard_map/ppermute | solution.py:124
  373.2 37.9 %copy-start.19 = (bf16[4,2,128,768]{3,2,1,0:T(8,128)(2,1)S(1)}, bf16[4,2,128,768]{3,2,1,0:T(8,128)(2,1)}, u32[]{:S(2)}) copy-start(bf16[4,2,128,768]{3,2,1,0:T(8,128)(2,1)} %convolution_convert_fusion.3) | copy-start | bytes 4718596
  373.2 131.6 %collective-permute-start.33 = (bf16[2,128,1024]{2,1,0:T(8,128)(2,1)}, bf16[2,128,1024]{2,1,0:T(8,128)(2,1)}, u32[]{:S(2)}, u32[]{:S(2)}) collective-permute-start(bf16[2,128,1024]{2,1,0:T(8,128)(2,1)} %dynamic-slice_bitcast_fusion.3), channel_id=1, source_target_pairs={{0,2},{1,3},{2,0},{3,1},{4,6},{5,7},{6,4},{7,5},{8,10},{9,11},{10,... | collective-permute-start | bytes 1572872 | tf_op jit(solution)/shard_map/ppermute | solution.py:124
  384.4 48.9 %collective-permute-start.55 = (bf16[128,1152]{1,0:T(8,128)(2,1)S(1)}, bf16[128,1152]{1,0:T(8,128)(2,1)S(1)}, u32[]{:S(2)}, u32[]{:S(2)}) collective-permute-start(bf16[128,1152]{1,0:T(8,128)(2,1)S(1)} %get-tuple-element.529), channel_id=1, source_target_pairs={{0,8},{8,16},{16,24},{24,0},{1,9},{9,17},{17,25},{25,1},{2,10},{10... | collective-permute-start | bytes 884744 | tf_op jit(solution)/shard_map/ppermute | solution.py:54
  407.9 28.7 %collective-permute-start.57 = (bf16[128,1152]{1,0:T(8,128)(2,1)S(1)}, bf16[128,1152]{1,0:T(8,128)(2,1)S(1)}, u32[]{:S(2)}, u32[]{:S(2)}) collective-permute-start(bf16[128,1152]{1,0:T(8,128)(2,1)S(1)} %get-tuple-element.530), channel_id=1, source_target_pairs={{0,24},{8,0},{16,8},{24,16},{1,25},{9,1},{17,9},{25,17},{2,26},{10... | collective-permute-start | bytes 884744 | tf_op jit(solution)/shard_map/ppermute | solution.py:54
  432.8 23.4 %collective-permute-start.56 = (bf16[128,1152]{1,0:T(8,128)(2,1)S(1)}, bf16[128,1152]{1,0:T(8,128)(2,1)S(1)}, u32[]{:S(2)}, u32[]{:S(2)}) collective-permute-start(bf16[128,1152]{1,0:T(8,128)(2,1)S(1)} %get-tuple-element.531), channel_id=1, source_target_pairs={{0,16},{8,24},{16,0},{24,8},{1,17},{9,25},{17,1},{25,9},{2,18},{10... | collective-permute-start | bytes 884744 | tf_op jit(solution)/shard_map/ppermute | solution.py:54
  433.3 23.8 %collective-permute-start.50 = (bf16[128,1152]{1,0:T(8,128)(2,1)S(1)}, bf16[128,1152]{1,0:T(8,128)(2,1)S(1)}, u32[]{:S(2)}, u32[]{:S(2)}) collective-permute-start(bf16[128,1152]{1,0:T(8,128)(2,1)S(1)} %get-tuple-element.526), channel_id=1, source_target_pairs={{0,8},{8,16},{16,24},{24,0},{1,9},{9,17},{17,25},{25,1},{2,10},{10... | collective-permute-start | bytes 884744 | tf_op jit(solution)/shard_map/ppermute | solution.py:54
  436.7 29.5 %collective-permute-start.52 = (bf16[128,1152]{1,0:T(8,128)(2,1)S(1)}, bf16[128,1152]{1,0:T(8,128)(2,1)S(1)}, u32[]{:S(2)}, u32[]{:S(2)}) collective-permute-start(bf16[128,1152]{1,0:T(8,128)(2,1)S(1)} %get-tuple-element.527), channel_id=1, source_target_pairs={{0,24},{8,0},{16,8},{24,16},{1,25},{9,1},{17,9},{25,17},{2,26},{10... | collective-permute-start | bytes 884744 | tf_op jit(solution)/shard_map/ppermute | solution.py:54
  456.2 24.4 %collective-permute-start.51 = (bf16[128,1152]{1,0:T(8,128)(2,1)S(1)}, bf16[128,1152]{1,0:T(8,128)(2,1)S(1)}, u32[]{:S(2)}, u32[]{:S(2)}) collective-permute-start(bf16[128,1152]{1,0:T(8,128)(2,1)S(1)} %get-tuple-element.528), channel_id=1, source_target_pairs={{0,16},{8,24},{16,0},{24,8},{1,17},{9,25},{17,1},{25,9},{2,18},{10... | collective-permute-start | bytes 884744 | tf_op jit(solution)/shard_map/ppermute | solution.py:54
  457.1 43.1 %copy-start.39 = (bf16[2,128,1152]{2,1,0:T(8,128)(2,1)}, bf16[2,128,1152]{2,1,0:T(8,128)(2,1)S(1)}, u32[]{:S(2)}) copy-start(bf16[2,128,1152]{2,1,0:T(8,128)(2,1)S(1)} %get-tuple-element.470) | copy-start | bytes 1769476
  457.1 24.4 %collective-permute-start.45 = (bf16[128,1152]{1,0:T(8,128)(2,1)S(1)}, bf16[128,1152]{1,0:T(8,128)(2,1)S(1)}, u32[]{:S(2)}, u32[]{:S(2)}) collective-permute-start(bf16[128,1152]{1,0:T(8,128)(2,1)S(1)} %get-tuple-element.523), channel_id=1, source_target_pairs={{0,8},{8,16},{16,24},{24,0},{1,9},{9,17},{17,25},{25,1},{2,10},{10... | collective-permute-start | bytes 884744 | tf_op jit(solution)/shard_map/ppermute | solution.py:54
  466.1 20.5 %collective-permute-start.47 = (bf16[128,1152]{1,0:T(8,128)(2,1)S(1)}, bf16[128,1152]{1,0:T(8,128)(2,1)S(1)}, u32[]{:S(2)}, u32[]{:S(2)}) collective-permute-start(bf16[128,1152]{1,0:T(8,128)(2,1)S(1)} %get-tuple-element.524), channel_id=1, source_target_pairs={{0,24},{8,0},{16,8},{24,16},{1,25},{9,1},{17,9},{25,17},{2,26},{10... | collective-permute-start | bytes 884744 | tf_op jit(solution)/shard_map/ppermute | solution.py:54
  480.5 18.8 %collective-permute-start.46 = (bf16[128,1152]{1,0:T(8,128)(2,1)S(1)}, bf16[128,1152]{1,0:T(8,128)(2,1)S(1)}, u32[]{:S(2)}, u32[]{:S(2)}) collective-permute-start(bf16[128,1152]{1,0:T(8,128)(2,1)S(1)} %get-tuple-element.525), channel_id=1, source_target_pairs={{0,16},{8,24},{16,0},{24,8},{1,17},{9,25},{17,1},{25,9},{2,18},{10... | collective-permute-start | bytes 884744 | tf_op jit(solution)/shard_map/ppermute | solution.py:54
  481.5 33.8 %collective-permute-start.58 = (bf16[128,1152]{1,0:T(8,128)(2,1)}, bf16[128,1152]{1,0:T(8,128)(2,1)}, u32[]{:S(2)}, u32[]{:S(2)}) collective-permute-start(bf16[128,1152]{1,0:T(8,128)(2,1)} %get-tuple-element.471), channel_id=1, source_target_pairs={{0,4},{4,0},{1,5},{5,1},{2,6},{6,2},{3,7},{7,3},{8,12},{12,8},{9,1... | collective-permute-start | bytes 884744 | tf_op jit(solution)/shard_map/ppermute | solution.py:54
  486.6 28.6 %collective-permute-start.53 = (bf16[128,1152]{1,0:T(8,128)(2,1)}, bf16[128,1152]{1,0:T(8,128)(2,1)}, u32[]{:S(2)}, u32[]{:S(2)}) collective-permute-start(bf16[128,1152]{1,0:T(8,128)(2,1)} %get-tuple-element.469), channel_id=1, source_target_pairs={{0,4},{4,0},{1,5},{5,1},{2,6},{6,2},{3,7},{7,3},{8,12},{12,8},{9,1... | collective-permute-start | bytes 884744 | tf_op jit(solution)/shard_map/ppermute | solution.py:54
  503.3 14.4 %collective-permute-start.48 = (bf16[128,1152]{1,0:T(8,128)(2,1)}, bf16[128,1152]{1,0:T(8,128)(2,1)S(1)}, u32[]{:S(2)}, u32[]{:S(2)}) collective-permute-start(bf16[128,1152]{1,0:T(8,128)(2,1)} %get-tuple-element.467), channel_id=1, source_target_pairs={{0,4},{4,0},{1,5},{5,1},{2,6},{6,2},{3,7},{7,3},{8,12},{12,8},{9,1... | collective-permute-start | bytes 884744 | tf_op jit(solution)/shard_map/ppermute | solution.py:54
  513.2 22.9 %collective-permute-start.34 = (bf16[2,128,1024]{2,1,0:T(8,128)(2,1)}, bf16[2,128,1024]{2,1,0:T(8,128)(2,1)}, u32[]{:S(2)}, u32[]{:S(2)}) collective-permute-start(bf16[2,128,1024]{2,1,0:T(8,128)(2,1)} %get-tuple-element.475), channel_id=1, source_target_pairs={{0,2},{1,3},{2,0},{3,1},{4,6},{5,7},{6,4},{7,5},{8,10},{9,11},{10,... | collective-permute-start | bytes 1572872 | tf_op jit(solution)/shard_map/ppermute | solution.py:136
  537.2 2.7 collective-permute-start.35
  609.1 17.0 %collective-permute-start.36 = (bf16[2,512,256]{1,0,2:T(2,128)(2,1)}, bf16[2,512,256]{1,0,2:T(2,128)(2,1)}, u32[]{:S(2)}, u32[]{:S(2)}) collective-permute-start(bf16[2,512,256]{1,0,2:T(2,128)(2,1)} %dynamic-slice_bitcast_fusion.2), channel_id=1, source_target_pairs={{0,4},{4,0},{1,5},{5,1},{2,6},{6,2},{3,7},{7,3},{8,12},{12,8},{9,1... | collective-permute-start | bytes 1572872 | tf_op jit(solution)/shard_map/ppermute | solution.py:54
  640.2 19.6 %collective-permute-start.39 = (bf16[4,128,768]{2,1,0:T(8,128)(2,1)}, bf16[4,128,768]{2,1,0:T(8,128)(2,1)}, u32[]{:S(2)}, u32[]{:S(2)}) collective-permute-start(bf16[4,128,768]{2,1,0:T(8,128)(2,1)} %fusion.126), channel_id=1, source_target_pairs={{0,4},{4,0},{1,5},{5,1},{2,6},{6,2},{3,7},{7,3},{8,12},{12,8},{9,1... | collective-permute-start | bytes 2359304 | tf_op jit(solution)/shard_map/ppermute | solution.py:54
  648.3 33.7 %collective-permute-start.37 = (bf16[2,2,128,1024]{3,2,0,1:T(8,128)(2,1)}, bf16[2,2,128,1024]{3,2,0,1:T(8,128)(2,1)}, u32[]{:S(2)}, u32[]{:S(2)}) collective-permute-start(bf16[2,2,128,1024]{3,2,0,1:T(8,128)(2,1)} %bitcast.560), channel_id=1, source_target_pairs={{0,1},{1,0},{2,3},{3,2},{4,5},{5,4},{6,7},{7,6},{8,9},{9,8},{10,11... | collective-permute-start | bytes 3145736 | tf_op jit(solution)/shard_map/ppermute | solution.py:117
  661.3 9.9 %collective-permute-start.40 = (bf16[128,768]{1,0:T(8,128)(2,1)S(1)}, bf16[128,768]{1,0:T(8,128)(2,1)S(1)}, u32[]{:S(2)}, u32[]{:S(2)}) collective-permute-start(bf16[128,768]{1,0:T(8,128)(2,1)S(1)} %get-tuple-element.543), channel_id=1, source_target_pairs={{0,8},{8,16},{16,24},{24,0},{1,9},{9,17},{17,25},{25,1},{2,10},{10... | collective-permute-start | bytes 589832 | tf_op jit(solution)/shard_map/ppermute | solution.py:54
  661.6 11.6 %collective-permute-start.42 = (bf16[128,768]{1,0:T(8,128)(2,1)S(1)}, bf16[128,768]{1,0:T(8,128)(2,1)S(1)}, u32[]{:S(2)}, u32[]{:S(2)}) collective-permute-start(bf16[128,768]{1,0:T(8,128)(2,1)S(1)} %get-tuple-element.544), channel_id=1, source_target_pairs={{0,24},{8,0},{16,8},{24,16},{1,25},{9,1},{17,9},{25,17},{2,26},{10... | collective-permute-start | bytes 589832 | tf_op jit(solution)/shard_map/ppermute | solution.py:54
  665.4 14.3 %collective-permute-start.41 = (bf16[128,768]{1,0:T(8,128)(2,1)S(1)}, bf16[128,768]{1,0:T(8,128)(2,1)S(1)}, u32[]{:S(2)}, u32[]{:S(2)}) collective-permute-start(bf16[128,768]{1,0:T(8,128)(2,1)S(1)} %get-tuple-element.545), channel_id=1, source_target_pairs={{0,16},{8,24},{16,0},{24,8},{1,17},{9,25},{17,1},{25,9},{2,18},{10... | collective-permute-start | bytes 589832 | tf_op jit(solution)/shard_map/ppermute | solution.py:54
  680.6 9.0 %collective-permute-start.43 = (bf16[128,768]{1,0:T(8,128)(2,1)}, bf16[128,768]{1,0:T(8,128)(2,1)}, u32[]{:S(2)}, u32[]{:S(2)}) collective-permute-start(bf16[128,768]{1,0:T(8,128)(2,1)} %get-tuple-element.473), channel_id=1, source_target_pairs={{0,4},{4,0},{1,5},{5,1},{2,6},{6,2},{3,7},{7,3},{8,12},{12,8},{9,1... | collective-permute-start | bytes 589832 | tf_op jit(solution)/shard_map/ppermute | solution.py:54
  685.5 20.2 %collective-permute-start.38 = (bf16[2,128,1024]{2,1,0:T(8,128)(2,1)}, bf16[2,128,1024]{2,1,0:T(8,128)(2,1)}, u32[]{:S(2)}, u32[]{:S(2)}) collective-permute-start(bf16[2,128,1024]{2,1,0:T(8,128)(2,1)} %dynamic-slice_bitcast_fusion.1), channel_id=1, source_target_pairs={{0,2},{1,3},{2,0},{3,1},{4,6},{5,7},{6,4},{7,5},{8,10},{9,11},{10,... | collective-permute-start | bytes 1572872 | tf_op jit(solution)/shard_map/ppermute | solution.py:124
  701.6 50.7 %copy-start.98 = (f32[2,128]{1,0:T(2,128)S(1)}, f32[2,128]{1,0:T(2,128)}, u32[]{:S(2)}) copy-start(f32[2,128]{1,0:T(2,128)} %copy-done.97) | copy-start | bytes 3076
  (117 other events, 684.2 us)
